TPU v7x, 256 devices: a whole 4x4x8 slice. The times are simulated.
256 devices in a mesh: lat: 2 (over core), lon: 128 (over z, y, x).
Axes of the slice: x: 4, y: 4, z: 8, core: 2. Of those that a mesh axis runs over, the one named last changes fastest.
Arguments:
- tracer: float32 [4, 5760, 2304], P(None, 'lon', 'lat'), may hold values from -6 to 6
- zonal_wind: float32 [4, 5760, 2304], P(None, 'lon', 'lat'), may hold values from -7.5 to 7.5
- meridional_wind: float32 [4, 5760, 2304], P(None, 'lon', 'lat'), may hold values from -6 to 6
- cutoffs: int32 [2, 384], replicated, may hold values from 1 to 127
Outputs:
- advected: float32 [4, 5760, 2304], P(None, 'lon', 'lat')
All inputs are finite; a program needn't handle non-finite values.
Results may differ from a plain program's by a relative error of at most 0.0001.
Values sent between devices are 32-bit elements; how exact they have to be, the bound alone decides.
A program may use at most 64 MiB of HBM per device.

v0:
```python
import math

import jax
import jax.numpy as jnp
from jax import lax
from jax.sharding import PartitionSpec as P

KMAX = 128
SUBSTEPS = 3


def extended(cells, sides, width, closed):
    for axis, dim in sides:
        count = lax.axis_size(axis)
        ends = count if closed else count - 1
        head = lax.slice_in_dim(cells, 0, width, axis=dim)
        tail = lax.slice_in_dim(cells, cells.shape[dim] - width, cells.shape[dim], axis=dim)
        cells = jnp.concatenate(
            [
                lax.ppermute(tail, axis, [(i, (i + 1) % count) for i in range(ends)]),
                cells,
                lax.ppermute(head, axis, [((i + 1) % count, i) for i in range(ends)]),
            ],
            axis=dim,
        )
    return cells


def passed_along(value, axis, steps):
    count = lax.axis_size(axis)
    pairs = [(source, (source + steps) % count) for source in range(count)]
    return lax.ppermute(value, axis, pairs)


def fourier_basis(columns, lon_total, mode_count):
    modes = jnp.arange(mode_count, dtype=jnp.int32)
    phase = columns[:, None] * modes[None, :] % lon_total
    angles = 2.0 * math.pi / lon_total * phase.astype(jnp.float32)
    return jnp.concatenate([jnp.cos(angles), jnp.sin(angles)], axis=1)


def mode_weights(lon_total, mode_count):
    modes = jnp.arange(mode_count, dtype=jnp.int32)
    base = jnp.where(modes == 0, 1.0, 2.0).astype(jnp.float32) / lon_total
    return jnp.concatenate([base, base])


def keep_mask(cuts, mode_count):
    modes = jnp.arange(mode_count, dtype=jnp.int32)
    both = jnp.concatenate([modes, modes])
    return (both[None, :] <= cuts[:, None]).astype(jnp.float32)


def body(tracer, zonal_wind, meridional_wind, cutoffs):
    lev_count, seg_width, row_count = tracer.shape
    lat_count = lax.axis_size("lat")
    lon_count = lax.axis_size("lon")
    lat_index = lax.axis_index("lat")
    lon_index = lax.axis_index("lon")
    lon_total = seg_width * lon_count
    lat_total = row_count * lat_count
    cap_rows = row_count // 3
    first_row = lat_index * row_count
    row_ids = first_row + jnp.arange(row_count, dtype=jnp.int32)
    colat = math.pi * (row_ids.astype(jnp.float32) + 0.5) / lat_total
    stretch = (1.0 / jnp.maximum(jnp.sin(colat), 0.125))[None, None, :]
    columns = lon_index * seg_width + jnp.arange(seg_width, dtype=jnp.int32)
    basis_cols = fourier_basis(columns, lon_total, KMAX)
    weights = mode_weights(lon_total, KMAX)
    north_cap = lat_index == 0
    south_cap = lat_index == lat_count - 1
    cap_start = jnp.where(north_cap, 0, row_count - cap_rows).astype(jnp.int32)
    chosen = jnp.where(north_cap, cutoffs[0], cutoffs[1])
    field = tracer
    for step in range(SUBSTEPS):
        padded = extended(field, (("lon", 1),), 1, True)
        eastern = padded[:, 2:, :]
        western = padded[:, :-2, :]
        banded = extended(field, (("lat", 2),), 1, False)
        edges = jnp.stack([field[:, :, 0], field[:, :, -1]], axis=2)
        opposite = passed_along(edges, "lon", lon_count // 2)
        top = jnp.where(north_cap, opposite[:, :, 0], banded[:, :, 0])
        bottom = jnp.where(south_cap, opposite[:, :, 1], banded[:, :, -1])
        northern = jnp.concatenate([top[:, :, None], field[:, :, :-1]], axis=2)
        southern = jnp.concatenate([field[:, :, 1:], bottom[:, :, None]], axis=2)
        tendency = (
            -0.05 * stretch * zonal_wind * (eastern - western)
            - 0.05 * meridional_wind * (northern - southern)
            + 0.02 * stretch * (eastern - 2.0 * field + western)
        )
        cap_slab = lax.dynamic_slice_in_dim(tendency, cap_start, cap_rows, 2)
        partial_value = jnp.einsum(
            "lsc,sk->lck",
            cap_slab,
            basis_cols,
            preferred_element_type=jnp.float32,
            precision=lax.Precision.HIGHEST,
        )
        coef = lax.psum(partial_value, "lon")
        scaled = coef * (keep_mask(chosen, KMAX) * weights[None, :])[None, :, :]
        filtered = jnp.einsum(
            "lck,sk->lsc",
            scaled,
            basis_cols,
            preferred_element_type=jnp.float32,
            precision=lax.Precision.HIGHEST,
        )
        tendency = lax.dynamic_update_slice_in_dim(tendency, filtered, cap_start, 2)
        field = field + tendency
    return field


def solution(mesh):
    placed = (P(None, "lon", "lat"), P(None, "lon", "lat"), P(None, "lon", "lat"), P())
    return jax.shard_map(
        body, mesh=mesh, in_specs=placed, out_specs=P(None, "lon", "lat"), check_vma=False
    )
```

profile of v0, /device:TPU:8, one launch (start us, length us, event | category | flops | bytes accessed | tf_op | source)
XLA Modules:
  0.0 773.3 jit_solution(6658652749218048721)
XLA Ops:
  7.4 2.6 collective-permute-start
  11.7 2.1 collective-permute-start.3
  14.4 1.3 collective-permute-start.4
  15.7 1.7 pad_maximum_fusion.6
  17.4 7.2 collective-permute-start.2
  26.4 1.2 collective-permute-done.2
  29.7 1.4 fusion.26
  31.2 3.6 fusion.40
  35.0 229.8 %all-reduce.4.cloned.1.call-done = f32[4,384,256]{2,1,0:T(8,128)} async-done(((f32[4,384,256]{2,1,0:T(8,128)}), f32[4,384,256]{2,1,0:T(8,128)}) %all-reduce.4.cloned.1.call-update) | async-done | bytes 1572880 | tf_op jit(solution)/shard_map/psum | solution.py:99
  264.9 3.7 fusion.9
  268.5 1.3 copy_add_fusion
  269.9 1.3 collective-permute-start.9
  271.3 3.0 collective-permute-start.8
  274.6 3.3 collective-permute-start.7
  278.0 2.8 collective-permute-start.5
  280.9 3.5 collective-permute-done.7
  284.5 2.2 collective-permute-done.6
  286.7 1.5 fusion.29
  288.3 3.6 fusion.38
  292.0 222.2 %all-reduce.6.cloned.1.call-done = f32[4,384,256]{2,1,0:T(8,128)} async-done(((f32[4,384,256]{2,1,0:T(8,128)}), f32[4,384,256]{2,1,0:T(8,128)}) %all-reduce.6.cloned.1.call-update) | async-done | bytes 1572880 | tf_op jit(solution)/shard_map/psum | solution.py:99
  514.2 3.7 fusion.15
  517.9 1.3 add.93
  519.2 1.3 collective-permute-start.14
  520.6 3.0 collective-permute-start.13
  523.9 3.3 collective-permute-start.12
  527.3 2.8 collective-permute-start.10
  530.2 3.5 collective-permute-done.12
  533.8 2.2 collective-permute-done.11
  537.6 2.6 fusion.36
  540.2 222.3 %all-reduce.8.cloned.1.call-done = f32[4,384,256]{2,1,0:T(8,128)} async-done(((f32[4,384,256]{2,1,0:T(8,128)}), f32[4,384,256]{2,1,0:T(8,128)}) %all-reduce.8.cloned.1.call-update) | async-done | bytes 1572880 | tf_op jit(solution)/shard_map/psum | solution.py:99
  762.5 3.0 fusion.21
  765.6 1.2 copy.88
  (77 shorter events, 10.3 us)
Async XLA Ops:
  6.5 18.1 %copy-start = (f32[4,45,1152]{2,0,1:T(4,128)S(1)}, f32[4,45,1152]{2,0,1:T(4,128)}, u32[]{:S(2)}) copy-start(f32[4,45,1152]{2,0,1:T(4,128)} %param.4) | copy-start | bytes 2488324
  6.5 258.3 %all-reduce.4.cloned.1.call-start = ((), (), s32[]{:S(2)}) async-start(), calls=%async_computation | async-start | bytes 3145728 | tf_op jit(solution)/shard_map/psum | solution.py:99
  7.4 21.3 %collective-permute-start = (f32[4,1,1152]{2,0,1:T(4,128)S(1)}, f32[4,1,1152]{2,0,1:T(4,128)}, u32[]{:S(2)}, u32[]{:S(2)}) collective-permute-start(f32[4,1,1152]{2,0,1:T(4,128)S(1)} %get-tuple-element.19), channel_id=1, source_target_pairs={{1,0},{2,1},{3,2},{4,3},{5,4},{6,5},{7,6},{8,7},{9,8},{10,9},{11,1... | collective-permute-start | bytes 55304 | tf_op jit(solution)/shard_map/ppermute | solution.py:22
  10.0 18.7 %collective-permute-start.1 = (f32[4,1,1152]{2,0,1:T(4,128)S(1)}, f32[4,1,1152]{2,0,1:T(4,128)}, u32[]{:S(2)}, u32[]{:S(2)}) collective-permute-start(f32[4,1,1152]{2,0,1:T(4,128)S(1)} %get-tuple-element.20), channel_id=1, source_target_pairs={{0,1},{1,2},{2,3},{3,4},{4,5},{5,6},{6,7},{7,8},{8,9},{9,10},{10,1... | collective-permute-start | bytes 55304 | tf_op jit(solution)/shard_map/ppermute | solution.py:20
  11.7 14.7 %collective-permute-start.3 = (f32[4,45,1]{2,1,0:T(8,128)}, f32[4,45,1]{2,1,0:T(8,128)}, u32[]{:S(2)}, u32[]{:S(2)}) collective-permute-start(f32[4,45,1]{2,1,0:T(8,128)} %copy.110), channel_id=1, source_target_pairs={{0,128},{1,129},{2,130},{3,131},{4,132},{5,133},{6,134},{7,135},{8... | collective-permute-start | bytes 2168 | tf_op jit(solution)/shard_map/ppermute | solution.py:20
  14.4 12.0 %collective-permute-start.4 = (f32[4,45,1]{2,1,0:T(8,128)}, f32[4,45,1]{2,1,0:T(8,128)}, u32[]{:S(2)}, u32[]{:S(2)}) collective-permute-start(f32[4,45,1]{2,1,0:T(8,128)} %copy.111), channel_id=1, source_target_pairs={{128,0},{129,1},{130,2},{131,3},{132,4},{133,5},{134,6},{135,7},{1... | collective-permute-start | bytes 2168 | tf_op jit(solution)/shard_map/ppermute | solution.py:22
  17.4 10.2 %collective-permute-start.2 = (f32[4,45,2]{2,1,0:T(8,128)}, f32[4,45,2]{2,1,0:T(8,128)}, u32[]{:S(2)}, u32[]{:S(2)}) collective-permute-start(f32[4,45,2]{2,1,0:T(8,128)} %pad_maximum_fusion.6), channel_id=1, source_target_pairs={{0,64},{1,65},{2,66},{3,67},{4,68},{5,69},{6,70},{7,71},{8,72},{9,... | collective-permute-start | bytes 4328 | tf_op jit(solution)/shard_map/ppermute | solution.py:32
  26.4 3.3 copy-start.1
  26.4 3.3 copy-start.2
  26.4 3.3 copy-start.8
  31.2 3.7 copy-start.9
  34.8 479.4 %all-reduce.6.cloned.1.call-start = ((), (), s32[]{:S(2)}) async-start(), calls=%async_computation.1 | async-start | bytes 3145728 | tf_op jit(solution)/shard_map/psum | solution.py:99
  35.0 229.8 %copy-start.3 = (f32[384,256]{1,0:T(8,128)}, f32[384,256]{1,0:T(8,128)S(1)}, u32[]{:S(2)}) copy-start(f32[384,256]{1,0:T(8,128)S(1)} %compare_select_fusion) | copy-start | bytes 1179652
  269.9 11.0 %collective-permute-start.9 = (f32[4,45,1]{2,1,0:T(8,128)S(1)}, f32[4,45,1]{2,1,0:T(8,128)S(1)}, u32[]{:S(2)}, u32[]{:S(2)}) collective-permute-start(f32[4,45,1]{2,1,0:T(8,128)S(1)} %get-tuple-element.15), channel_id=1, source_target_pairs={{128,0},{129,1},{130,2},{131,3},{132,4},{133,5},{134,6},{135,7},{1... | collective-permute-start | bytes 2168 | tf_op jit(solution)/shard_map/ppermute | solution.py:22
  271.3 9.6 %collective-permute-start.8 = (f32[4,45,1]{2,1,0:T(8,128)S(1)}, f32[4,45,1]{2,1,0:T(8,128)S(1)}, u32[]{:S(2)}, u32[]{:S(2)}) collective-permute-start(f32[4,45,1]{2,1,0:T(8,128)S(1)} %get-tuple-element.16), channel_id=1, source_target_pairs={{0,128},{1,129},{2,130},{3,131},{4,132},{5,133},{6,134},{7,135},{8... | collective-permute-start | bytes 2168 | tf_op jit(solution)/shard_map/ppermute | solution.py:20
  274.6 9.7 %collective-permute-start.7 = (f32[4,45,2]{2,1,0:T(8,128)S(1)}, f32[4,45,2]{2,1,0:T(8,128)S(1)}, u32[]{:S(2)}, u32[]{:S(2)}) collective-permute-start(f32[4,45,2]{2,1,0:T(8,128)S(1)} %pad_maximum_fusion.7), channel_id=1, source_target_pairs={{0,64},{1,65},{2,66},{3,67},{4,68},{5,69},{6,70},{7,71},{8,72},{9,... | collective-permute-start | bytes 4328 | tf_op jit(solution)/shard_map/ppermute | solution.py:32
  278.0 6.4 collective-permute-start.5
  280.8 5.9 collective-permute-start.6
  288.3 225.9 %copy-start.4 = (f32[384,256]{1,0:T(8,128)S(1)}, f32[384,256]{1,0:T(8,128)}, u32[]{:S(2)}) copy-start(f32[384,256]{1,0:T(8,128)} %copy-done.3) | copy-start | bytes 1179652
  291.9 470.6 %all-reduce.8.cloned.1.call-start = ((), (), s32[]{:S(2)}) async-start(), calls=%async_computation.2 | async-start | bytes 3145728 | tf_op jit(solution)/shard_map/psum | solution.py:99
  519.2 11.0 %collective-permute-start.14 = (f32[4,45,1]{2,1,0:T(8,128)S(1)}, f32[4,45,1]{2,1,0:T(8,128)S(1)}, u32[]{:S(2)}, u32[]{:S(2)}) collective-permute-start(f32[4,45,1]{2,1,0:T(8,128)S(1)} %get-tuple-element.9), channel_id=1, source_target_pairs={{128,0},{129,1},{130,2},{131,3},{132,4},{133,5},{134,6},{135,7},{1... | collective-permute-start | bytes 2168 | tf_op jit(solution)/shard_map/ppermute | solution.py:22
  520.6 9.6 %collective-permute-start.13 = (f32[4,45,1]{2,1,0:T(8,128)S(1)}, f32[4,45,1]{2,1,0:T(8,128)S(1)}, u32[]{:S(2)}, u32[]{:S(2)}) collective-permute-start(f32[4,45,1]{2,1,0:T(8,128)S(1)} %get-tuple-element.10), channel_id=1, source_target_pairs={{0,128},{1,129},{2,130},{3,131},{4,132},{5,133},{6,134},{7,135},{8... | collective-permute-start | bytes 2168 | tf_op jit(solution)/shard_map/ppermute | solution.py:20
  523.9 9.7 %collective-permute-start.12 = (f32[4,45,2]{2,1,0:T(8,128)S(1)}, f32[4,45,2]{2,1,0:T(8,128)S(1)}, u32[]{:S(2)}, u32[]{:S(2)}) collective-permute-start(f32[4,45,2]{2,1,0:T(8,128)S(1)} %pad_maximum_fusion.8), channel_id=1, source_target_pairs={{0,64},{1,65},{2,66},{3,67},{4,68},{5,69},{6,70},{7,71},{8,72},{9,... | collective-permute-start | bytes 4328 | tf_op jit(solution)/shard_map/ppermute | solution.py:32
  527.3 6.4 collective-permute-start.10
  530.2 5.9 collective-permute-start.11
  536.7 0.9 copy-start.6
  537.6 224.9 %copy-start.5 = (f32[384,256]{1,0:T(8,128)S(1)}, f32[384,256]{1,0:T(8,128)}, u32[]{:S(2)}) copy-start(f32[384,256]{1,0:T(8,128)} %copy-done.3) | copy-start | bytes 1179652
  540.2 222.3 %copy-start.7 = (f32[4,45,1152]{2,1,0:T(8,128)S(1)}, f32[4,45,1152]{2,1,0:T(8,128)}, u32[]{:S(2)}) copy-start(f32[4,45,1152]{2,1,0:T(8,128)} %copy-done.6) | copy-start | bytes 2488324
Sparse Core Ops, SparseCore 0:
  34.9 229.9 all-reduce.3
  292.0 222.0 all-reduce.5
  540.3 222.1 all-reduce.7
where the time goes:
time: 774 us; the launch traced here: 773 us
  waiting for transfers between devices  687 us (89%)
  starting transfers between devices  34.3 us (4%)
  matrix products  20.1 us (3%)
  between operations  13.5 us (2%)
  other arithmetic  10.7 us (1%)
  local copies, waits for them, and re-layouts  7.77 us (1%)
    psum x3, waiting for transfers between devices, body(): coef = lax.psum(partial_value, 'lon')  674 us
  transfers between devices with their start and end apart: 18, of which 8 were waited for; matrix products, arithmetic and copies ran while one was open for 1% of the time, Pallas kernels for 0%

commit v1 on v0

v1 whole, which is shorter than its diff:
```python
import functools
import math

import jax
import jax.numpy as jnp
import numpy as np
from jax import lax
from jax.sharding import PartitionSpec as P

KMAX = 128
CHUNK = 12
WIN = 16
HI = lax.Precision.HIGHEST


def tables(seg, segs):
    total = seg * segs
    k = np.arange(KMAX)
    s = np.arange(segs)
    c = np.arange(seg)
    a = 2 * np.pi * ((k[None, :] * s[:, None]) % segs) / segs
    b = 2 * np.pi * (k[None, :] * c[:, None]) / total
    w = np.where(k == 0, 1.0, 2.0) / total
    f32 = lambda x: np.asarray(x, np.float32)
    return f32(np.cos(a)), f32(np.sin(a)), f32(np.cos(b)), f32(np.sin(b)), f32(w)


def stretch_of(rows, lat_total):
    colat = math.pi * (rows.astype(jnp.float32) + 0.5) / lat_total
    return 1.0 / jnp.maximum(jnp.sin(colat), 0.125)


def tend(mid, east, west, north, south, u, v, s):
    return (
        -0.05 * s * u * (east - west)
        - 0.05 * v * (north - south)
        + 0.02 * s * (east - 2.0 * mid + west)
    )


def body(f, u, v, cutoffs):
    lev, seg, rows = f.shape
    segs = lax.axis_size("lon")
    lat_total = rows * lax.axis_size("lat")
    lat = lax.axis_index("lat")
    lon = lax.axis_index("lon")
    south = lat == 1
    cap = rows // 3
    per = lev * cap // (CHUNK * lev)
    xs = cap + 4
    left = [(i, (i - 1) % segs) for i in range(segs)]
    right = [(i, (i + 1) % segs) for i in range(segs)]
    opposite = [(i, (i + segs // 2) % segs) for i in range(segs)]

    head = jnp.concatenate([f[:, :3], u[:, :2], v[:, :2]], axis=1)
    tail = jnp.concatenate([f[:, -3:], u[:, -2:], v[:, -2:]], axis=1)
    east = lax.ppermute(head, "lon", left)
    west = lax.ppermute(tail, "lon", right)
    edge = lax.ppermute(jnp.where(south, f[:, :, -1], f[:, :, 0]), "lon", opposite)[:, :, None]
    fx = jnp.concatenate([west[:, :3], f, east[:, :3]], axis=1)
    ux = jnp.concatenate([west[:, 3:5], u, east[:, 3:5]], axis=1)
    vx = jnp.concatenate([west[:, 5:], v, east[:, 5:]], axis=1)

    fc = fx[:, 2:-2]
    pad = jnp.pad(edge, ((0, 0), (1, 1), (0, 0)))
    fc = jnp.where(
        south,
        jnp.concatenate([fc[:, :, rows - xs - 1 :], pad], axis=2),
        jnp.concatenate([pad, fc[:, :, : xs + 1]], axis=2),
    )
    cut_rows = lambda a: jnp.where(south, a[:, :, rows - xs :], a[:, :, :xs])
    uc, vc = cut_rows(u), cut_rows(v)
    row0 = jnp.where(south, lat_total - xs, 0)
    sc = stretch_of(row0 + jnp.arange(xs), lat_total)
    t1 = tend(
        fc[:, 1:-1, 1:-1], fc[:, 2:, 1:-1], fc[:, :-2, 1:-1],
        fc[:, 1:-1, :-2], fc[:, 1:-1, 2:], uc, vc, sc,
    )
    sent = jnp.stack([t1, uc, vc], axis=1).transpose(0, 3, 1, 2)
    idx = np.arange(per)[:, None] * CHUNK + np.arange(WIN)[None, :]
    sent = sent[:, idx].reshape(lev * per, WIN, 3, seg)
    got = lax.all_to_all(sent, "lon", 0, 0, tiled=True)
    got = got.transpose(2, 1, 3, 0)
    t1, uw, vw = got[0], got[1], got[2]

    jj = lon % per
    x = jj * CHUNK + jnp.arange(WIN)
    sw = stretch_of(row0 + x, lat_total)[:, None, None]
    in_cap = jnp.where(south, x >= 4, x < cap)
    cut_at = jnp.clip(jnp.where(south, x - 4, x), 0, cap - 1)
    cuts = jnp.where(south, cutoffs[1], cutoffs[0])[cut_at]
    ca, sa, cb, sb, w = tables(seg, segs)
    fwd = np.concatenate([ca, sa], axis=1)
    keep = (jnp.arange(KMAX)[None, :] <= cuts[:, None]) * w[None, :]
    north_pole = (~south) & (jj == 0)
    south_pole = south & (jj == per - 1)

    def filt(t):
        z = jnp.einsum("tcs,sk->tck", t, fwd, precision=HI)
        zc, zs = z[:, :, :KMAX], z[:, :, KMAX:]
        a = jnp.sum(cb * zc - sb * zs, axis=1) * keep
        b = jnp.sum(cb * zs + sb * zc, axis=1) * keep
        a, b = a[:, None], b[:, None]
        d = jnp.concatenate([a * cb + b * sb, b * cb - a * sb], axis=2)
        y = jnp.einsum("tck,sk->tcs", d, fwd, precision=HI)
        return jnp.where(in_cap[:, None, None], y, t)

    def lap(g):
        e = jnp.concatenate([g[:, 1:], jnp.roll(g[:, :1], -1, axis=2)], axis=1)
        ww = jnp.concatenate([jnp.roll(g[:, -1:], 1, axis=2), g[:, :-1]], axis=1)
        half = segs // 2
        first = jnp.where(north_pole, jnp.roll(g[:1], half, axis=2), g[:1])
        last = jnp.where(south_pole, jnp.roll(g[-1:], half, axis=2), g[-1:])
        n = jnp.concatenate([first, g[:-1]], axis=0)
        s = jnp.concatenate([g[1:], last], axis=0)
        return tend(g, e, ww, n, s, uw, vw, sw)

    g = filt(t1)
    g = g + filt(t1 + lap(g))
    g = g + filt(t1 + lap(g))
    back = lax.all_to_all(g.transpose(2, 0, 1), "lon", 0, 0, tiled=True)
    back = back.reshape(lev, per, WIN, seg)
    mid_rows = back[:, :, 2 : 2 + CHUNK].reshape(lev, cap, seg)
    add = jnp.concatenate([back[:, 0, :2], mid_rows, back[:, -1, 14:]], axis=1).transpose(0, 2, 1)

    def edges(a, n):
        return jnp.where(south, a[:, :, :n], a[:, :, rows - n :])

    swap = [(0, 1), (1, 0)]
    halo = lax.ppermute(
        jnp.concatenate([edges(fx, 3), jnp.pad(edges(ux, 2), ((0, 0), (1, 1), (0, 0))), jnp.pad(edges(vx, 2), ((0, 0), (1, 1), (0, 0)))], axis=2),
        "lat", swap,
    )
    fh, uh, vh = halo[:, :, :3], halo[:, 1:-1, 3:5], halo[:, 1:-1, 5:]

    def middle(a, h, extra):
        n = 2 * cap + extra
        return jnp.where(
            south,
            jnp.concatenate([h, a[:, :, :n]], axis=2),
            jnp.concatenate([a[:, :, rows - n :], h], axis=2),
        )

    fm, um, vm = middle(fx, fh, 1), middle(ux, uh, 0), middle(vx, vh, 0)
    first = jnp.where(south, rows - 2, cap)
    sm = stretch_of(first + jnp.arange(2 * cap + 2), lat_total)
    for step in range(3):
        t = tend(
            fm[:, 1:-1, 1:-1], fm[:, 2:, 1:-1], fm[:, :-2, 1:-1],
            fm[:, 1:-1, :-2], fm[:, 1:-1, 2:], um, vm, sm,
        )
        fm = fm[:, 1:-1, 1:-1] + t
        um, vm, sm = um[:, 1:-1, 1:-1], vm[:, 1:-1, 1:-1], sm[1:-1]

    n_out = jnp.concatenate([f[:, :, : cap + 2] + add[:, :, : cap + 2], fm], axis=2)
    s_out = jnp.concatenate([fm, f[:, :, rows - cap - 2 :] + add[:, :, 2:]], axis=2)
    return jnp.where(south, s_out, n_out)


def solution(mesh):
    placed = (P(None, "lon", "lat"), P(None, "lon", "lat"), P(None, "lon", "lat"), P())
    return jax.shard_map(
        body, mesh=mesh, in_specs=placed, out_specs=P(None, "lon", "lat"), check_vma=False
    )
```

time: 774 us -> 124 us (0.16)
  waiting for transfers between devices: 687 us -> 32.1 us
  local copies, waits for them, and re-layouts: 7.77 us -> 34 us
  matrix products: 20.1 us -> 4.68 us
  between operations: 13.5 us -> 0.76 us
  other arithmetic: 10.7 us -> 21.2 us
    psum x3 -> x0, waiting for transfers between devices: 674 us -> none  [body(): coef = lax.psum(partial_value, 'lon')]
    all_to_all x0 -> x2, waiting for transfers between devices: none -> 32 us  [the longest x1 23.7 us: body(): got = lax.all_to_all(sent, 'lon', 0, 0, tiled=True)]
    ppermute x15 -> x4, starting transfers between devices: 34.2 us -> 11.7 us  [the longest x1 7.23 us: body(): lax.ppermute(jnp.where(south, f[:, :, -1], f[:, :, 0]), 'lon', opposite)]
    all_to_all x0 -> x2, starting transfers between devices: none -> 18.7 us  [the longest x1 12.3 us: body(): got = lax.all_to_all(sent, 'lon', 0, 0, tiled=True)]
    dot_general x6, matrix products: 20.1 us -> 4.68 us  [the longest x3 2.37 us: filt(): y = jnp.einsum('tck,sk->tcs', d, fwd, precision=HI)]
    ppermute x15 -> x4, waiting for transfers between devices: 12.6 us -> 0.01 us  [the longest x1 0.01 us: body(): lax.ppermute(jnp.where(south, f[:, :, -1], f[:, :, 0]), 'lon', opposite)]
    unnamed x24 -> x59, local copies, waits for them, and re-layouts: 3.28 us -> 14 us
  transfers between devices with their start and end apart: 18 -> 6, of which waited for: 8 -> 2; matrix products, arithmetic and copies ran while one was open for 1% -> 12% of each run, Pallas kernels for 0% -> 0%
where the time goes in v1:
time: 124 us; the launch traced here: 123 us
  local copies, waits for them, and re-layouts  34 us (27%)
  waiting for transfers between devices  32.1 us (26%)
  starting transfers between devices  30.4 us (25%)
  other arithmetic  21.2 us (17%)
  matrix products  4.68 us (4%)
    all_to_all x1, waiting for transfers between devices, body(): got = lax.all_to_all(sent, 'lon', 0, 0, tiled=True)  23.7 us
    unnamed x59, local copies, waits for them, and re-layouts  14 us
    all_to_all x1, starting transfers between devices, body(): got = lax.all_to_all(sent, 'lon', 0, 0, tiled=True)  12.3 us
    all_to_all x1, waiting for transfers between devices, body(): back = lax.all_to_all(g.transpose(2, 0, 1), 'lon', 0, 0, tiled=True)  8.34 us
    ppermute x1, starting transfers between devices, body(): lax.ppermute(jnp.where(south, f[:, :, -1], f[:, :, 0]), 'lon', opposite)  7.23 us
    add x3, other arithmetic, body(): fm = fm[:, 1:-1, 1:-1] + t  7.19 us
    all_to_all x1, starting transfers between devices, body(): back = lax.all_to_all(g.transpose(2, 0, 1), 'lon', 0, 0, tiled=True)  6.44 us
    gather x2, local copies, waits for them, and re-layouts, body(): sent = sent[:, idx].reshape(lev * per, WIN, 3, seg)  6.15 us
  transfers between devices with their start and end apart: 6, of which 2 were waited for; matrix products, arithmetic and copies ran while one was open for 12% of the time, Pallas kernels for 0%

profile of v1, /device:TPU:8, one launch (start us, length us, event | category | flops | bytes accessed | tf_op | source)
XLA Modules:
  0.0 123.2 jit_solution(3011370093682830433)
XLA Ops:
  0.0 0.9 fusion.57
  0.9 0.8 fusion.58
  1.8 1.6 %collective-permute-start = (f32[4,7,1152]{2,0,1:T(4,128)S(1)}, f32[4,7,1152]{2,0,1:T(4,128)S(1)}, u32[]{:S(2)}, u32[]{:S(2)}) collective-permute-start(f32[4,7,1152]{2,0,1:T(4,128)S(1)} %pad_maximum_fusion.6), channel_id=1, source_target_pairs={{0,1},{1,2},{2,3},{3,4},{4,5},{5,6},{6,7},{7,8},{8,9},{9,10},{10,1... | collective-permute-start | bytes 387080 | tf_op jit(solution)/shard_map/ppermute | solution.py:58
  3.4 2.7 %collective-permute-start.1 = (f32[4,7,1152]{2,0,1:T(4,128)S(1)}, f32[4,7,1152]{2,0,1:T(4,128)S(1)}, u32[]{:S(2)}, u32[]{:S(2)}) collective-permute-start(f32[4,7,1152]{2,0,1:T(4,128)S(1)} %pad_maximum_fusion.7), channel_id=1, source_target_pairs={{0,127},{1,0},{2,1},{3,2},{4,3},{5,4},{6,5},{7,6},{8,7},{9,8},{10,... | collective-permute-start | bytes 387080 | tf_op jit(solution)/shard_map/ppermute | solution.py:57
  6.4 7.2 %collective-permute-start.3 = (f32[4,45]{1,0:T(4,128)S(1)}, f32[4,45]{1,0:T(4,128)S(1)}, u32[]{:S(2)}, u32[]{:S(2)}) collective-permute-start(f32[4,45]{1,0:T(4,128)S(1)} %bitcast.73), channel_id=1, source_target_pairs={{0,64},{1,65},{2,66},{3,67},{4,68},{5,69},{6,70},{7,71},{8,72},{9,... | collective-permute-start | bytes 2168 | tf_op jit(solution)/shard_map/ppermute | solution.py:59
  15.6 0.8 pad_maximum_fusion.8
  18.3 1.2 fusion.40
  19.9 1.5 %copy.144 = f32[4,3,45,388]{2,0,1,3:T(4,128)S(1)} copy(f32[4,3,45,388]{3,0,2,1:T(4,128)S(1)} %pad_maximum_fusion) | data formatting | bytes 1676160 | tf_op jit(solution)/shard_map/stack | solution.py:79
  21.3 4.0 %gather_fusion = f32[512,4,3,45]{3,1,2,0:T(4,128)} fusion(f32[4,388,3,45]{3,0,2,1:T(4,128)S(1)} %bitcast.62, s32[1024]{0:T(1024)S(1)} %pad_clamp_fusion.1), kind=kCustom, calls=%fused_computation | custom fusion | bytes 2213888 | tf_op jit(solution)/shard_map/gather | solution.py:81
  25.3 2.2 %copy.145 = f32[512,4,3,45]{3,0,2,1:T(8,128)S(1)} copy(f32[512,4,3,45]{3,1,2,0:T(4,128)} %gather_fusion) | data formatting | bytes 2211840 | tf_op jit(solution)/shard_map/gather | solution.py:81
  27.7 4.2 %reshape.291 = f32[128,1,2160]{2,1,0:T(1,128)} reshape(f32[128,3,16,45]{3,2,1,0:T(8,128)S(1)} %bitcast.68) | data formatting | bytes 2211840
  32.0 12.3 %all-to-all-start = ((f32[128,1,2160]{2,1,0:T(1,128)}), f32[128,1,2160]{2,1,0:T(1,128)S(1)}, u32[]{:S(2)}, u32[]{:S(2)}) async-start(f32[128,1,2160]{2,1,0:T(1,128)} %reshape.291), calls=%async_computation | async-start | bytes 2228224 | tf_op jit(solution)/shard_map/all_to_all | solution.py:82
  46.5 1.2 fusion.55
  48.5 1.1 fusion.56
  50.0 0.8 copy.139
  51.3 23.7 %all-to-all-done = f32[128,1,2160]{2,1,0:T(1,128)S(1)} async-done(((f32[128,1,2160]{2,1,0:T(1,128)}), f32[128,1,2160]{2,1,0:T(1,128)S(1)}, u32[]{:S(2)}, u32[]{:S(2)}) %all-to-all-start) | async-done | bytes 1105952 | tf_op jit(solution)/shard_map/all_to_all | solution.py:82
  75.6 3.3 %reduce.2 = f32[128,2160]{1,0:T(8,128)S(1)} reduce(f32[128,1,2160]{2,1,0:T(1,128)S(1)} %all-to-all-done, f32[]{:T(128)} %broadcast.440), dimensions={1}, to_apply=%all_to_all.6.reduce_sub_computation | reduce | bytes 2211844 | tf_op jit(solution)/shard_map/all_to_all | solution.py:82
  78.9 3.4 %reshape.292 = f32[128,3,16,45]{3,2,1,0:T(8,128)} reshape(f32[128,2160]{1,0:T(8,128)S(1)} %reduce.2) | data formatting | bytes 2211840
  82.3 2.4 %copy.148 = f32[128,16,3,45]{0,3,1,2:T(8,128)S(1)} copy(f32[128,16,3,45]{3,1,2,0:T(8,128)} %bitcast.69) | data formatting | bytes 2211840 | tf_op jit(solution)/shard_map/all_to_all | solution.py:82
  84.8 0.8 fusion.43
  85.9 0.8 convolution_select_fusion.2
  87.9 0.8 fusion.73
  89.0 0.8 fusion.2
  91.6 0.8 fusion.1
  93.0 2.1 %reshape.293 = f32[128,1,720]{2,1,0:T(1,128)} reshape(f32[128,16,45]{2,1,0:T(8,128)S(1)} %copy.149) | data formatting | bytes 737280
  95.1 6.4 %all-to-all-start.1 = ((f32[128,1,720]{2,1,0:T(1,128)}), f32[128,1,720]{2,1,0:T(1,128)S(1)}, u32[]{:S(2)}, u32[]{:S(2)}) async-start(f32[128,1,720]{2,1,0:T(1,128)} %reshape.293), calls=%async_computation.1 | async-start | bytes 786432 | tf_op jit(solution)/shard_map/all_to_all | solution.py:121
  101.5 3.6 %fusion.15 = (f32[4,49,770]{2,0,1:T(4,128)S(1)}, f32[4,49,770]{2,0,1:T(4,128)S(1)}, f32[4,49,770]{2,0,1:T(4,128)S(1)}) fusion(f32[4,51,772]{2,0,1:T(4,128)S(1)} %maximum_select_fusion.1, f32[770]{0:T(1024)S(1)} %get-tuple-element.94, f32[770]{0:T(1024)S(1)} %broadcast_multiply_fusion.1, f32[4,49,2]{2,0,1:T(4,128)S(1)} %copy.137, ...), kind=kLoop, calls=%fused_computation.27 | loop fusion | flops 2867480 | bytes 7247185 | tf_op jit(solution)/shard_map/add | solution.py:152
  105.1 1.9 %fusion.19 = f32[4,47,768]{2,0,1:T(4,128)S(1)} fusion(f32[4,49,770]{2,0,1:T(4,128)S(1)} %get-tuple-element.11, f32[4,49,770]{2,0,1:T(4,128)S(1)} %get-tuple-element.13, f32[4,49,770]{2,0,1:T(4,128)S(1)} %get-tuple-element.12, f32[768]{0:T(1024)S(1)} %get-tuple-element.80, f32[768]{0:T(1024)S(1)} %get-tuple-element.79), kind=kLoop, calls=%fused_computation.34 | loop fusion | flops 1876992 | bytes 4626432 | tf_op jit(solution)/shard_map/add | solution.py:152
  107.0 1.8 %fusion.24 = f32[4,45,766]{2,0,1:T(4,128)S(1)} fusion(f32[4,47,768]{2,0,1:T(4,128)S(1)} %fusion.19, f32[4,49,770]{2,0,1:T(4,128)S(1)} %get-tuple-element.13, f32[4,49,770]{2,0,1:T(4,128)S(1)} %get-tuple-element.12, f32[766]{0:T(1024)S(1)} %get-tuple-element.78, f32[766]{0:T(1024)S(1)} %get-tuple-element.77), kind=kLoop, calls=%fused_computation.42 | loop fusion | flops 1792440 | bytes 4418288 | tf_op jit(solution)/shard_map/add | solution.py:152
  108.8 8.3 %all-to-all-done.1 = f32[128,1,720]{2,1,0:T(1,128)S(1)} async-done(((f32[128,1,720]{2,1,0:T(1,128)}), f32[128,1,720]{2,1,0:T(1,128)S(1)}, u32[]{:S(2)}, u32[]{:S(2)}) %all-to-all-start.1) | async-done | bytes 368672 | tf_op jit(solution)/shard_map/all_to_all | solution.py:121
  117.1 1.6 %reduce.3 = f32[128,720]{1,0:T(8,128)S(1)} reduce(f32[128,1,720]{2,1,0:T(1,128)S(1)} %all-to-all-done.1, f32[]{:T(128)} %broadcast.440), dimensions={1}, to_apply=%all_to_all.7.reduce_sub_computation | reduce | bytes 737284 | tf_op jit(solution)/shard_map/all_to_all | solution.py:121
  121.7 1.5 %maximum_select_fusion = f32[4,45,1152]{2,0,1:T(4,128)} fusion(f32[4,45,386]{2,0,1:T(4,128)S(1)} %get-tuple-element.15, f32[4,45,766]{2,0,1:T(4,128)S(1)} %fusion.24, f32[4,45,386]{2,0,1:T(4,128)S(1)} %get-tuple-element.14, pred[]{:T(512)S(6)} %eq.11), kind=kLoop, calls=%fused_computation.12 | loop fusion | flops 622080 | bytes 1936801 | tf_op jit(solution)/shard_map/jit(_where)/select_n | solution.py:157
  (133 shorter events, 16.1 us)
Async XLA Ops:
  0.0 13.9 %copy-start.24 = (s32[512]{0:T(512)S(1)}, s32[512]{0:T(512)}, u32[]{:S(2)}) copy-start(s32[512]{0:T(512)} %constant.130) | copy-start | bytes 6148
  0.0 6.2 %copy-start.2 = (f32[4,45,1152]{2,0,1:T(4,128)S(1)}, f32[4,45,1152]{2,0,1:T(4,128)}, u32[]{:S(2)}) copy-start(f32[4,45,1152]{2,0,1:T(4,128)} %param.15) | copy-start | bytes 2488324
  0.0 14.0 %copy-start.23 = (s32[2,384]{1,0:T(2,128)S(1)}, s32[2,384]{1,0:T(2,128)}, u32[]{:S(2)}) copy-start(s32[2,384]{1,0:T(2,128)} %param.18) | copy-start | bytes 9220
  1.8 13.7 %collective-permute-start = (f32[4,7,1152]{2,0,1:T(4,128)S(1)}, f32[4,7,1152]{2,0,1:T(4,128)S(1)}, u32[]{:S(2)}, u32[]{:S(2)}) collective-permute-start(f32[4,7,1152]{2,0,1:T(4,128)S(1)} %pad_maximum_fusion.6), channel_id=1, source_target_pairs={{0,1},{1,2},{2,3},{3,4},{4,5},{5,6},{6,7},{7,8},{8,9},{9,10},{10,1... | collective-permute-start | bytes 387080 | tf_op jit(solution)/shard_map/ppermute | solution.py:58
  3.4 12.1 %collective-permute-start.1 = (f32[4,7,1152]{2,0,1:T(4,128)S(1)}, f32[4,7,1152]{2,0,1:T(4,128)S(1)}, u32[]{:S(2)}, u32[]{:S(2)}) collective-permute-start(f32[4,7,1152]{2,0,1:T(4,128)S(1)} %pad_maximum_fusion.7), channel_id=1, source_target_pairs={{0,127},{1,0},{2,1},{3,2},{4,3},{5,4},{6,5},{7,6},{8,7},{9,8},{10,... | collective-permute-start | bytes 387080 | tf_op jit(solution)/shard_map/ppermute | solution.py:57
  6.4 9.0 %collective-permute-start.3 = (f32[4,45]{1,0:T(4,128)S(1)}, f32[4,45]{1,0:T(4,128)S(1)}, u32[]{:S(2)}, u32[]{:S(2)}) collective-permute-start(f32[4,45]{1,0:T(4,128)S(1)} %bitcast.73), channel_id=1, source_target_pairs={{0,64},{1,65},{2,66},{3,67},{4,68},{5,69},{6,70},{7,71},{8,72},{9,... | collective-permute-start | bytes 2168 | tf_op jit(solution)/shard_map/ppermute | solution.py:59
  15.5 1.0 copy-start.16
  15.6 1.0 copy-start.18
  16.6 1.0 copy-start
  16.6 1.5 %copy-start.4 = (f32[4,45,1152]{2,0,1:T(4,128)S(1)}, f32[4,45,1152]{2,0,1:T(4,128)}, u32[]{:S(2)}) copy-start(f32[4,45,1152]{2,0,1:T(4,128)} %param.17) | copy-start | bytes 2488324
  16.6 1.7 %copy-start.6 = (f32[4,45,1152]{2,0,1:T(4,128)S(1)}, f32[4,45,1152]{2,0,1:T(4,128)}, u32[]{:S(2)}) copy-start(f32[4,45,1152]{2,0,1:T(4,128)} %param.16) | copy-start | bytes 2488324
  32.0 12.3 %copy-start.17 = (f32[4,7,1152]{2,0,1:T(4,128)S(1)}, f32[4,7,1152]{2,0,1:T(4,128)}, u32[]{:S(2)}) copy-start(f32[4,7,1152]{2,0,1:T(4,128)} %copy-done.16) | copy-start | bytes 387076
  32.0 12.3 %copy-start.19 = (f32[4,7,1152]{2,0,1:T(4,128)S(1)}, f32[4,7,1152]{2,0,1:T(4,128)}, u32[]{:S(2)}) copy-start(f32[4,7,1152]{2,0,1:T(4,128)} %copy-done.18) | copy-start | bytes 387076
  32.0 12.4 %copy-start.7 = (f32[4,45,1152]{2,0,1:T(4,128)S(1)}, f32[4,45,1152]{2,0,1:T(4,128)}, u32[]{:S(2)}) copy-start(f32[4,45,1152]{2,0,1:T(4,128)} %param.16) | copy-start | bytes 2488324
  32.0 43.0 %all-to-all-start = ((f32[128,1,2160]{2,1,0:T(1,128)}), f32[128,1,2160]{2,1,0:T(1,128)S(1)}, u32[]{:S(2)}, u32[]{:S(2)}) async-start(f32[128,1,2160]{2,1,0:T(1,128)} %reshape.291), calls=%async_computation | async-start | bytes 2228224 | tf_op jit(solution)/shard_map/all_to_all | solution.py:82
  44.3 0.9 copy-start.15
  44.3 1.0 copy-start.14
  44.3 1.2 %copy-start.5 = (f32[4,45,1152]{2,0,1:T(4,128)S(1)}, f32[4,45,1152]{2,0,1:T(4,128)}, u32[]{:S(2)}) copy-start(f32[4,45,1152]{2,0,1:T(4,128)} %param.17) | copy-start | bytes 2488324
  45.8 3.8 %collective-permute-start.2 = (f32[4,51,7]{1,0,2:T(4,128)S(1)}, f32[4,51,7]{1,0,2:T(4,128)S(1)}, u32[]{:S(2)}, u32[]{:S(2)}) collective-permute-start(f32[4,51,7]{1,0,2:T(4,128)S(1)} %select_maximum_fusion), channel_id=1, source_target_pairs={{0,128},{128,0},{1,129},{129,1},{2,130},{130,2},{3,131},{131,3},{4... | collective-permute-start | bytes 17144 | tf_op jit(solution)/shard_map/ppermute | solution.py:130
  46.5 1.6 %copy-start.1 = (f32[4,51,1152]{2,0,1:T(4,128)S(1)}, f32[4,51,1152]{2,0,1:T(4,128)}, u32[]{:S(2)}) copy-start(f32[4,51,1152]{2,0,1:T(4,128)} %copy-done) | copy-start | bytes 2820100
  82.3 2.5 %copy-start.8 = (f32[128,256,1]{1,0,2:T(8,128)S(1)}, f32[128,256,1]{1,0,2:T(8,128)}, u32[]{:S(2)}) copy-start(f32[128,256,1]{1,0,2:T(8,128)} %constant.131) | copy-start | bytes 393220
  84.7 0.8 copy-start.12
  84.8 0.8 copy-start.13
  84.8 1.0 copy-start.20
  86.8 0.7 copy-start.21
  86.9 0.7 copy-start.22
  93.0 8.5 %copy-start.9 = (f32[4,49,768]{2,0,1:T(4,128)S(1)}, f32[4,49,768]{2,0,1:T(4,128)}, u32[]{:S(2)}) copy-start(f32[4,49,768]{2,0,1:T(4,128)} %get-tuple-element.24) | copy-start | bytes 1806340
  93.0 8.5 %copy-start.10 = (f32[4,49,768]{2,0,1:T(4,128)S(1)}, f32[4,49,768]{2,0,1:T(4,128)}, u32[]{:S(2)}) copy-start(f32[4,49,768]{2,0,1:T(4,128)} %get-tuple-element.25) | copy-start | bytes 1806340
  95.1 6.5 %copy-start.11 = (f32[4,49,768]{2,0,1:T(4,128)S(1)}, f32[4,49,768]{2,0,1:T(4,128)}, u32[]{:S(2)}) copy-start(f32[4,49,768]{2,0,1:T(4,128)} %get-tuple-element.26) | copy-start | bytes 1806340
  95.1 22.0 %all-to-all-start.1 = ((f32[128,1,720]{2,1,0:T(1,128)}), f32[128,1,720]{2,1,0:T(1,128)S(1)}, u32[]{:S(2)}, u32[]{:S(2)}) async-start(f32[128,1,720]{2,1,0:T(1,128)} %reshape.293), calls=%async_computation.1 | async-start | bytes 786432 | tf_op jit(solution)/shard_map/all_to_all | solution.py:121
  120.1 1.2 copy-start.3

commit v2 on v0

v2 whole, which is shorter than its diff:
```python
import functools
import math

import jax
import jax.numpy as jnp
import ml_dtypes
import numpy as np
from jax import lax
from jax.experimental import pallas as pl
from jax.experimental.pallas import tpu as pltpu
from jax.sharding import PartitionSpec as P

MESH = pl.DeviceIdType.MESH
LEV, SEG, ROWS, SEGS = 4, 45, 1152, 128
CAP = ROWS // 3
CHUNK, WIN = 12, 16
PER = CAP // CHUNK
CW = 512
SHIFT = CW - CAP - 4
MW = 1024
KMAX = 128
C8 = 48
TAIL = 7
F32, BF16 = jnp.float32, jnp.bfloat16


def split(x):
    hi = x.astype(ml_dtypes.bfloat16)
    return hi, (x - hi.astype(np.float32)).astype(ml_dtypes.bfloat16)


def tables():
    total = SEG * SEGS
    k, s, c = np.arange(KMAX), np.arange(SEGS), np.arange(SEG)
    a = 2 * np.pi * ((s[:, None] * k[None, :]) % SEGS) / SEGS
    b = 2 * np.pi * (c[:, None] * k[None, :]) / total
    fwd = np.concatenate([np.cos(a), np.sin(a)], axis=1).astype(np.float32)
    pad = ((0, C8 - SEG), (0, 0))
    cb = np.pad(np.cos(b), pad).astype(np.float32)
    sb = np.pad(np.sin(b), pad).astype(np.float32)
    w = (np.where(k == 0, 1.0, 2.0) / total).astype(np.float32)[None, :]
    return split(fwd) + split(np.ascontiguousarray(fwd.T)) + (cb, sb, w)


def stretch_table():
    colat = np.float32(math.pi) * (np.arange(2 * ROWS).astype(np.float32) + np.float32(0.5))
    colat = (colat / np.float32(2 * ROWS)).astype(np.float32)
    s = np.float32(1.0) / np.maximum(np.sin(colat), np.float32(0.125))
    s = np.pad(s.astype(np.float32), (0, MW))
    cap = np.stack([s[:CW], s[2 * ROWS - CW : 2 * ROWS]])[:, None, :]
    mid = np.stack([s[256 : 256 + MW], s[ROWS - 128 : ROWS - 128 + MW]])[:, None, :]
    rows = np.stack([s[: CAP + 4], s[2 * ROWS - CAP - 4 : 2 * ROWS]])
    return cap, mid, rows


def tend(mid, east, west, north, south, u, v, s):
    return (
        -0.05 * s * u * (east - west)
        - 0.05 * v * (north - south)
        + 0.02 * s * (east - 2.0 * mid + west)
    )


def dot3(x, hi_ref, lo_ref):
    hi = x.astype(BF16)
    lo = (x - hi.astype(F32)).astype(BF16)
    dot = functools.partial(jnp.dot, preferred_element_type=F32)
    return dot(hi, hi_ref[...]) + (dot(lo, hi_ref[...]) + dot(hi, lo_ref[...]))


def kernel(
    f, u, v, cuts, rows_s, cap_s, mid_s, fh, fl, ih, il, cb_ref, sb_ref, w_ref,
    out,
    edge_w, edge_e, edge_o, got_w, got_e, got_o, mid_w, mid_e, mgot_w, mgot_e,
    fm, um, vm, fb, mm, mx, ln, lx, msg, recv, ext, ext_got, sp,
    tt, uu, vv, gg, xt, zz, dd, sb128, ret, back, rl,
    hs, hr, ms, mr, ls, lr, a_s, a_r, x_s, x_r, b_s, b_r,
):
    lat = lax.axis_index("lat")
    lon = lax.axis_index("lon")
    south = lat == 1
    jj = lax.rem(lon, PER)
    north_pole = jnp.logical_and(lat == 0, jj == 0)
    south_pole = jnp.logical_and(lat == 1, jj == PER - 1)
    at = lambda d: (lat, d)
    east_dev = at(lax.rem(lon + 1, SEGS))
    west_dev = at(lax.rem(lon + SEGS - 1, SEGS))
    opp_dev = at(lax.rem(lon + SEGS // 2, SEGS))
    partner = (1 - lat, lon)

    barrier = pltpu.get_barrier_semaphore()

    @pl.loop(1, SEGS)
    def _(k):
        pl.semaphore_signal(barrier, inc=1, device_id=at(lax.rem(lon + k, SEGS)), device_id_type=MESH)

    pl.semaphore_signal(barrier, inc=1, device_id=partner, device_id_type=MESH)

    cap0 = pl.multiple_of(lat * (ROWS - CW), 128)
    mid0 = pl.multiple_of((1 - lat) * 256, 128)
    edge0 = pl.multiple_of(lat * (ROWS - 128), 128)
    lane = lax.broadcasted_iota(jnp.int32, (C8, 128), 1)

    edge_o[...] = jnp.zeros_like(edge_o)
    edge_w[...] = jnp.zeros_like(edge_w)
    edge_e[...] = jnp.zeros_like(edge_e)
    mid_w[...] = jnp.zeros_like(mid_w)
    mid_e[...] = jnp.zeros_like(mid_e)
    for l in range(LEV):
        edge_w[l : l + 1] = f[l, 0:1, pl.ds(cap0, CW)]
        edge_e[l : l + 1] = f[l, SEG - 1 : SEG, pl.ds(cap0, CW)]
        tile = pltpu.roll(f[l, :, pl.ds(edge0, 128)], l + lat, 1)
        edge_o[0:SEG] = jnp.where(lane[:SEG] == l, tile, edge_o[0:SEG])
        for a, ref, n in ((0, f, 3), (3, u, 2), (5, v, 2)):
            mid_w[l, a : a + n] = ref[l, 0:n, pl.ds(mid0, MW - 128)]
            mid_e[l, a : a + n] = ref[l, SEG - n : SEG, pl.ds(mid0, MW - 128)]

    pl.semaphore_wait(barrier, SEGS)

    def remote(src, dst, send, recv_sem, dev):
        return pltpu.make_async_remote_copy(
            src_ref=src, dst_ref=dst, send_sem=send, recv_sem=recv_sem,
            device_id=dev, device_id_type=MESH,
        )

    halos = [
        remote(edge_w, got_e, hs.at[0], hr.at[0], west_dev),
        remote(edge_e, got_w, hs.at[1], hr.at[1], east_dev),
        remote(edge_o, got_o, hs.at[2], hr.at[2], opp_dev),
    ]
    mids = [
        remote(mid_w, mgot_e, ms.at[0], mr.at[0], west_dev),
        remote(mid_e, mgot_w, ms.at[1], mr.at[1], east_dev),
    ]
    for c in halos:
        c.start()
    for c in mids:
        c.start()
    for c in halos:
        c.wait()

    lanes = lax.broadcasted_iota(jnp.int32, (C8, CW), 1)
    scap = cap_s[lat]

    @pl.loop(0, LEV)
    def _(l):
        fb[8 : 8 + SEG] = f[l, :, pl.ds(cap0, CW)]
        fb[7:8] = got_w[pl.ds(l, 1)]
        fb[8 + SEG : 9 + SEG] = got_e[pl.ds(l, 1)]
        mid = fb[8 : 8 + C8]
        o = pltpu.roll(got_o[...], lax.rem(lat * 127 - l + 128, 128), 1)
        o = jnp.concatenate([o, o, o, o], axis=1)
        n = jnp.where(jnp.logical_and(lanes == 0, lat == 0), o, pltpu.roll(mid, 1, 1))
        s = jnp.where(jnp.logical_and(lanes == CW - 1, lat == 1), o, pltpu.roll(mid, CW - 1, 1))
        uc = u[l, :, pl.ds(cap0, CW)]
        vc = v[l, :, pl.ds(cap0, CW)]
        t1 = tend(mid[:SEG], fb[9 : 9 + SEG], fb[7 : 7 + SEG], n[:SEG], s[:SEG], uc, vc, scap)
        turn = lax.rem(CW - lat * SHIFT, CW)
        mm[0:SEG] = pltpu.roll(t1, turn, 1)
        mm[SEG : 2 * SEG] = pltpu.roll(uc, turn, 1)
        mm[2 * SEG : 3 * SEG] = pltpu.roll(vc, turn, 1)
        vt = mm[128 : 128 + TAIL]
        x12 = lax.rem(lanes[:TAIL], 12)
        mx[...] = mm[0:128]
        for i in range(8):
            t0 = i + 1 if i < 7 else 15
            t15 = i + 8 if i < 7 else 0
            a0 = pltpu.roll(vt, CW - t0, 1)
            a15 = pltpu.roll(vt, 15 - t15, 1)
            mx[SEG + TAIL * i : SEG + TAIL * (i + 1)] = jnp.where(x12 == 3, a15, a0)
        for b in range(CW // 128):
            ln[128 * b : 128 * (b + 1)] = mm[0:128, 128 * b : 128 * (b + 1)].T
            lx[128 * b : 128 * (b + 1)] = mx[0:128, 128 * b : 128 * (b + 1)].T
        row = lax.broadcasted_iota(jnp.int32, (WIN, 128), 0)

        @pl.loop(0, PER // 2)
        def _(m):
            a = ln[pl.ds(pl.multiple_of(24 * m, 8), 32)]
            b = lx[pl.ds(pl.multiple_of(24 * m, 8), 32)]
            first = jnp.logical_and(m == 0, lat == 0)
            last = jnp.logical_and(m == PER // 2 - 1, lat == 1)
            use0 = jnp.logical_or(jnp.logical_and(row == 0, jnp.logical_not(first)), row == WIN - 1)
            use1 = jnp.logical_or(row == 0, jnp.logical_and(row == WIN - 1, jnp.logical_not(last)))
            msg[l * PER + 2 * m] = jnp.where(use0, b[0:16], a[0:16])
            msg[l * PER + 2 * m + 1] = jnp.where(use1, b[12:28], a[12:28])

        ext[l] = jnp.where(lat == 0, lx[0:8], lx[PER * CHUNK - CHUNK + 8 : PER * CHUNK - CHUNK + 16])

    recv[lon] = msg[lon]

    def send_line(d):
        return remote(msg.at[d], recv.at[lon], a_s, a_r, at(d))

    @pl.loop(1, SEGS // 2)
    def _(k):
        send_line(lax.rem(lon + k, SEGS)).start()
        send_line(lax.rem(lon + SEGS - k, SEGS)).start()

    send_line(lax.rem(lon + SEGS // 2, SEGS)).start()

    def send_ext(l):
        d = l * PER + lat * (PER - 1)
        return d, remote(ext.at[l], ext_got.at[lon], x_s.at[l], x_r, at(d))

    for l in range(LEV):
        d, c = send_ext(l)

        @pl.when(d != lon)
        def _():
            c.start()

        @pl.when(d == lon)
        def _():
            ext_got[lon] = ext[l]

    for c in mids:
        c.wait()
    own = pl.multiple_of(lat * 128, 128)

    @pl.loop(0, LEV)
    def _(l):
        for ref, src, a, n in ((fm, f, 0, 3), (um, u, 3, 2), (vm, v, 5, 2)):
            ref[l, 3 : 3 + SEG, pl.ds(own, MW - 128)] = src[l, :, pl.ds(mid0, MW - 128)]
            ref[l, 3 - n : 3, pl.ds(own, MW - 128)] = mgot_w[l, a : a + n]
            ref[l, 3 + SEG : 3 + SEG + n, pl.ds(own, MW - 128)] = mgot_e[l, a : a + n]

    src0 = pl.multiple_of((1 - lat) * (MW - 256) + lat * 128, 128)
    dst0 = pl.multiple_of(lat * (MW - 128), 128)
    lats = [
        remote(ref.at[:, :, pl.ds(src0, 128)], ref.at[:, :, pl.ds((1 - lat) * 0 + dst0, 128)], ls.at[i], lr.at[i], partner)
        for i, ref in enumerate((fm, um, vm))
    ]
    for c in lats:
        c.start()
    for c in lats:
        c.wait()
    smid = mid_s[lat]

    @pl.loop(0, LEV)
    def _(l):
        for _ in range(3):
            x = fm[l]
            t = tend(
                x, pltpu.roll(x, 55, 0), pltpu.roll(x, 1, 0),
                pltpu.roll(x, 1, 1), pltpu.roll(x, MW - 1, 1), um[l], vm[l], smid,
            )
            fm[l] = x + t

    def total(sem, ref, n):
        pltpu.make_async_copy(ref.at[pl.ds(0, n)], ref.at[pl.ds(0, n)], sem).wait()

    total(a_r, recv, SEGS - 1)
    tt[:, SEG:C8] = jnp.zeros((WIN, C8 - SEG, 128), F32)
    uu[:, SEG:C8] = jnp.zeros((WIN, C8 - SEG, 128), F32)
    vv[:, SEG:C8] = jnp.zeros((WIN, C8 - SEG, 128), F32)
    for t in range(WIN):
        w = recv[:, t, :].T
        tt[t, 0:SEG] = w[0:SEG]
        uu[t, 0:SEG] = w[SEG : 2 * SEG]
        vv[t, 0 : SEG - TAIL] = w[2 * SEG : 128]
        if t == 0:
            sp[0] = w
        if t == WIN - 1:
            sp[1] = w

    @pl.when(jnp.logical_or(north_pole, south_pole))
    def _():
        total(x_r, ext_got, SEGS - 1)

    @pl.when(north_pole)
    def _():
        sp[0] = ext_got[:, 0, :].T

    @pl.when(south_pole)
    def _():
        sp[1] = ext_got[:, 7, :].T

    for i in range(8):
        t0 = i + 1 if i < 7 else 15
        t15 = i + 8 if i < 7 else 0
        lo, hi = SEG + TAIL * i, SEG + TAIL * (i + 1)
        vv[t0, SEG - TAIL : SEG] = sp[0, lo:hi]
        vv[t15, SEG - TAIL : SEG] = sp[1, lo:hi]

    col = lax.broadcasted_iota(jnp.int32, (C8, 128), 0)
    k_lane = lax.broadcasted_iota(jnp.int32, (1, KMAX), 1)
    cb, sb = cb_ref[...], sb_ref[...]

    for step in range(3):
        if step == 0:
            x_all = tt[...]
        else:

            @pl.loop(0, WIN)
            def _(t):
                g = gg[t]
                g8 = pltpu.roll(g[0:8], 127, 1)
                g40 = pltpu.roll(g[40:48], 1, 1)
                e = jnp.where(col == SEG - 1, jnp.broadcast_to(g8[0:1], (C8, 128)), pltpu.roll(g, C8 - 1, 0))
                w = jnp.where(col == 0, jnp.broadcast_to(g40[4:5], (C8, 128)), pltpu.roll(g, 1, 0))
                flip = pltpu.roll(g, SEGS // 2, 1)
                n = jnp.where(jnp.logical_and(north_pole, t == 0), flip, gg[jnp.maximum(t - 1, 0)])
                s = jnp.where(jnp.logical_and(south_pole, t == WIN - 1), flip, gg[jnp.minimum(t + 1, WIN - 1)])
                sw = rows_s[lat, CHUNK * jj + t]
                xt[t] = tt[t] + tend(g, e, w, n, s, uu[t], vv[t], sw)

            x_all = xt[...]
        x_all = x_all.reshape(WIN * C8, 128)
        zz[...] = dot3(x_all, fh, fl).reshape(WIN, C8, 2 * KMAX)

        @pl.loop(0, WIN)
        def _(t):
            zc, zs = zz[t, :, 0:KMAX], zz[t, :, KMAX:]
            x = CHUNK * jj + t - 4 * lat
            cut = cuts[lat, jnp.minimum(jnp.maximum(x, 0), CAP - 1)]
            keep = jnp.where(k_lane <= cut, w_ref[...], 0.0)
            a = jnp.sum(cb * zc - sb * zs, axis=0, keepdims=True) * keep
            b = jnp.sum(cb * zs + sb * zc, axis=0, keepdims=True) * keep
            dd[t, :, 0:KMAX] = a * cb + b * sb
            dd[t, :, KMAX:] = b * cb - a * sb

        zz[:, :, 0:128] = dot3(dd[...].reshape(WIN * C8, 2 * KMAX), ih, il).reshape(WIN, C8, 128)

        @pl.loop(0, WIN)
        def _(t):
            x = CHUNK * jj + t - 4 * lat
            inside = jnp.logical_and(x >= 0, x < CAP)
            raw = tt[t] if step == 0 else xt[t]
            y = jnp.where(inside, zz[t, :, 0:128], raw)
            gg[t] = y if step == 0 else gg[t] + y

    sb128[...] = jnp.zeros_like(sb128)
    for p in range(8):
        tb = 10 + p if p < 4 else (0, 1, 14, 15)[p - 4]
        sb128[0:C8] = gg[2 + p]
        sb128[64 : 64 + C8] = gg[tb]
        ret[:, p, :] = sb128[...].T

    back[lon] = ret[lon]

    def send_back(d):
        return remote(ret.at[d], back.at[lon], b_s, b_r, at(d))

    @pl.loop(1, SEGS // 2)
    def _(k):
        send_back(lax.rem(lon + k, SEGS)).start()
        send_back(lax.rem(lon + SEGS - k, SEGS)).start()

    send_back(lax.rem(lon + SEGS // 2, SEGS)).start()

    @pl.loop(0, LEV)
    def _(l):
        out[l, :, pl.ds(mid0, MW - 128)] = fm[l, 3 : 3 + SEG, pl.ds(own, MW - 128)]

    total(b_r, back, SEGS - 1)
    row8 = lax.broadcasted_iota(jnp.int32, (8, 128), 0)

    @pl.loop(0, LEV)
    def _(l):
        rl[CAP:CW] = jnp.zeros((CW - CAP, 128), F32)

        @pl.loop(0, PER // 2)
        def _(m):
            a0, a1 = back[l * PER + 2 * m], back[l * PER + 2 * m + 1]
            b0, b1 = pltpu.roll(a0, 64, 1), pltpu.roll(a1, 64, 1)
            a1r = pltpu.roll(a1, 4, 0)
            base = pl.multiple_of(24 * m + 8, 8)
            rl[pl.ds(base, 8)] = a0
            rl[pl.ds(pl.multiple_of(base + 8, 8), 8)] = jnp.where(row8 < 4, b0, a1r)
            rl[pl.ds(pl.multiple_of(base + 16, 8), 8)] = jnp.where(row8 < 4, a1r, pltpu.roll(b1, 4, 0))

        rl[0:8] = pltpu.roll(pltpu.roll(back[l * PER], 64, 1), 2, 0)
        rl[CAP + 8 : CAP + 16] = pltpu.roll(pltpu.roll(back[l * PER + PER - 1], 64, 1), 2, 0)
        add = jnp.concatenate([rl[128 * b : 128 * (b + 1)].T[0:C8] for b in range(CW // 128)], axis=1)
        add = pltpu.roll(add, lax.rem(lat * SHIFT + CW - 6, CW), 1)[0:SEG]
        x = lanes[:SEG] - lat * SHIFT
        inside = jnp.logical_and(x >= 2 * lat, x < CAP + 2 + 2 * lat)
        old = out[l, :, pl.ds(cap0, CW)]
        out[l, :, pl.ds(cap0, CW)] = jnp.where(inside, f[l, :, pl.ds(cap0, CW)] + add, old)

    total(a_s, msg, SEGS - 1)
    total(b_s, ret, SEGS - 1)
    for l in range(LEV):
        d, c = send_ext(l)

        @pl.when(d != lon)
        def _():
            c.wait_send()


def body(f, u, v, cutoffs):
    cap_s, mid_s, rows_s = stretch_table()
    vmem = pl.BlockSpec(memory_space=pltpu.VMEM)
    smem = pl.BlockSpec(memory_space=pltpu.SMEM)
    V = lambda *shape: pltpu.VMEM(shape, F32)
    dma = pltpu.SemaphoreType.DMA
    return pl.pallas_call(
        kernel,
        out_shape=jax.ShapeDtypeStruct(f.shape, F32),
        in_specs=[vmem] * 3 + [smem] * 2 + [vmem] * 9,
        out_specs=vmem,
        scratch_shapes=[
            V(8, CW), V(8, CW), V(C8, 128), V(8, CW), V(8, CW), V(C8, 128),
            V(LEV, 8, MW - 128), V(LEV, 8, MW - 128), V(LEV, 8, MW - 128), V(LEV, 8, MW - 128),
            V(LEV, 56, MW), V(LEV, 56, MW), V(LEV, 56, MW),
            V(64, CW), V(136, CW), V(128, CW), V(CW, 128), V(CW, 128),
            V(SEGS, WIN, 128), V(SEGS, WIN, 128), V(LEV, 8, 128), V(SEGS, 8, 128), V(2, 128, 128),
            V(WIN, C8, 128), V(WIN, C8, 128), V(WIN, C8, 128), V(WIN, C8, 128), V(WIN, C8, 128),
            V(WIN, C8, 256), V(WIN, C8, 256), V(128, 128), V(SEGS, 8, 128), V(SEGS, 8, 128), V(CW, 128),
            dma((3,)), dma((3,)), dma((2,)), dma((2,)), dma((3,)), dma((3,)),
            dma, dma, dma((LEV,)), dma, dma, dma,
        ],
        compiler_params=pltpu.CompilerParams(
            collective_id=0, has_side_effects=True, vmem_limit_bytes=40 * 1024 * 1024
        ),
    )(f, u, v, cutoffs, rows_s, cap_s, mid_s, *tables())


def solution(mesh):
    placed = (P(None, "lon", "lat"), P(None, "lon", "lat"), P(None, "lon", "lat"), P())
    return jax.shard_map(
        body, mesh=mesh, in_specs=placed, out_specs=P(None, "lon", "lat"), check_vma=False
    )
```

time: 774 us -> 80 us (0.10)
  waiting for transfers between devices: 687 us -> 0 us
  Pallas kernels: 0 us -> 74.3 us
  starting transfers between devices: 34.3 us -> 0 us
  matrix products: 20.1 us -> 0 us
  between operations: 13.5 us -> 0.12 us
  other arithmetic: 10.7 us -> 0 us
    psum x3 -> x0, waiting for transfers between devices: 674 us -> none  [body(): coef = lax.psum(partial_value, 'lon')]
    pallas_call x0 -> x1, Pallas kernels: none -> 74.3 us  [body(): pl.pallas_call(kernel, out_shape=jax.ShapeDtypeStruct(f.shape, F32), in_s...]
    ppermute x15 -> x0, starting transfers between devices: 34.2 us -> none  [the longest x3 13.8 us: passed_along(): return lax.ppermute(value, axis, pairs)]
    dot_general x6 -> x0, matrix products: 20.1 us -> none  [the longest x3 10.3 us: body(): jnp.einsum('lck,sk->lsc', scaled, basis_cols, preferred_element_type=jnp....]
    ppermute x15 -> x0, waiting for transfers between devices: 12.6 us -> none  [the longest x3 8.12 us: passed_along(): return lax.ppermute(value, axis, pairs)]
  transfers between devices with their start and end apart: 18 -> 0, of which waited for: 8 -> 0; matrix products, arithmetic and copies ran while one was open for 1% -> 0% of each run, Pallas kernels for 0% -> 0%
where the time goes in v2:
time: 80 us; the launch traced here: 79 us
  Pallas kernels  74.3 us (93%)
  local copies, waits for them, and re-layouts  4.63 us (6%)
    pallas_call x1, Pallas kernels, body(): pl.pallas_call(kernel, out_shape=jax.ShapeDtypeStruct(f.shape, F32), in_s...  74.3 us
    unnamed x29, local copies, waits for them, and re-layouts  3.42 us

profile of v2, /device:TPU:8, one launch (start us, length us, event | category | flops | bytes accessed | tf_op | source)
XLA Modules:
  0.0 79.0 jit_solution(14838067638007831098)
XLA Ops:
  0.0 0.0 copy-start.11
  0.0 1.3 %copy.15.f = f32[4,45,1152]{2,1,0:T(8,128)S(1)} copy(f32[4,45,1152]{2,0,1:T(4,128)} %param.14) | data formatting | bytes 1658880 | tf_op args[0]
  1.3 0.1 copy-done.11
  1.4 0.0 copy-start.12
  1.4 0.1 copy.16.u
  1.5 1.1 %copy-done.12 = f32[4,45,1152]{2,0,1:T(4,128)S(1)} copy-done((f32[4,45,1152]{2,0,1:T(4,128)S(1)}, f32[4,45,1152]{2,0,1:T(4,128)}, u32[]{:S(2)}) %copy-start.12) | copy-done | bytes 829464
  2.5 0.0 copy-start
  2.5 0.0 copy-start.1
  2.6 0.0 copy-start.2
  2.6 0.0 copy-start.3
  2.6 0.0 copy-start.4
  2.6 0.0 copy-start.5
  2.6 0.0 copy-start.6
  2.6 0.0 copy-start.7
  2.6 0.0 copy-start.8
  2.6 0.0 copy-start.9
  2.6 0.0 copy-start.10
  2.6 0.1 copy.17.v
  2.7 0.7 copy-done
  3.4 0.0 copy-done.1
  3.4 0.0 copy-done.2
  3.4 0.0 copy-done.3
  3.5 0.0 copy-done.4
  3.5 0.0 copy-done.5
  3.5 0.0 copy-done.6
  3.5 0.0 copy-done.7
  3.5 0.0 copy-done.8
  3.5 0.0 copy-done.9
  3.5 0.0 copy-done.10
  3.5 74.3 %shard_map.136 = f32[4,45,1152]{2,1,0:T(8,128)S(1)} custom-call(f32[4,45,1152]{2,1,0:T(8,128)S(1)} %copy.15.f, f32[4,45,1152]{2,1,0:T(8,128)S(1)} %copy.16.u, f32[4,45,1152]{2,1,0:T(8,128)S(1)} %copy.17.v, s32[2,384]{1,0:T(2,128)S(1)} %copy-done.9, f32[2,388]{1,0:T(2,128)S(1)} %copy-done.8, f32[2,1,512]{2,1,0:T(1,128)S(1)} %copy-done.7, ...), custom_call_target="tpu_custom_call" | custom-call | tf_op jit(solution)/shard_map/pallas_call | solution.py:397
  77.8 1.2 %copy.18 = f32[4,45,1152]{2,0,1:T(4,128)} copy(f32[4,45,1152]{2,1,0:T(8,128)S(1)} %shard_map.136) | data formatting | bytes 1658880 | tf_op jit(solution)/shard_map/pallas_call | solution.py:397
Async XLA Ops:
  0.0 1.4 %copy-start.11 = (f32[4,45,1152]{2,0,1:T(4,128)S(1)}, f32[4,45,1152]{2,0,1:T(4,128)}, u32[]{:S(2)}) copy-start(f32[4,45,1152]{2,0,1:T(4,128)} %param.15) | copy-start | bytes 2488324
  1.4 1.1 %copy-start.12 = (f32[4,45,1152]{2,0,1:T(4,128)S(1)}, f32[4,45,1152]{2,0,1:T(4,128)}, u32[]{:S(2)}) copy-start(f32[4,45,1152]{2,0,1:T(4,128)} %param.16) | copy-start | bytes 2488324
  2.5 0.8 %copy-start = (bf16[256,128]{1,0:T(8,128)(2,1)S(1)}, bf16[256,128]{1,0:T(8,128)(2,1)}, u32[]{:S(2)}) copy-start(bf16[256,128]{1,0:T(8,128)(2,1)} %constant.26.clone.il) | copy-start | bytes 196612
  2.5 0.9 %copy-start.1 = (bf16[256,128]{1,0:T(8,128)(2,1)S(1)}, bf16[256,128]{1,0:T(8,128)(2,1)}, u32[]{:S(2)}) copy-start(bf16[256,128]{1,0:T(8,128)(2,1)} %constant.25.clone.ih) | copy-start | bytes 196612
  2.6 0.9 %copy-start.2 = (bf16[128,256]{1,0:T(8,128)(2,1)S(1)}, bf16[128,256]{1,0:T(8,128)(2,1)}, u32[]{:S(2)}) copy-start(bf16[128,256]{1,0:T(8,128)(2,1)} %constant.24.clone.fl) | copy-start | bytes 196612
  2.6 0.9 %copy-start.3 = (bf16[128,256]{1,0:T(8,128)(2,1)S(1)}, bf16[128,256]{1,0:T(8,128)(2,1)}, u32[]{:S(2)}) copy-start(bf16[128,256]{1,0:T(8,128)(2,1)} %constant.23.clone.fh) | copy-start | bytes 196612
  2.6 0.9 %copy-start.4 = (f32[48,128]{1,0:T(8,128)S(1)}, f32[48,128]{1,0:T(8,128)}, u32[]{:S(2)}) copy-start(f32[48,128]{1,0:T(8,128)} %constant.28.clone.sb_ref) | copy-start | bytes 73732
  2.6 0.9 %copy-start.5 = (f32[48,128]{1,0:T(8,128)S(1)}, f32[48,128]{1,0:T(8,128)}, u32[]{:S(2)}) copy-start(f32[48,128]{1,0:T(8,128)} %constant.27.clone.cb_ref) | copy-start | bytes 73732
  2.6 0.9 %copy-start.6 = (f32[2,1,1024]{2,1,0:T(1,128)S(1)}, f32[2,1,1024]{2,1,0:T(1,128)}, u32[]{:S(2)}) copy-start(f32[2,1,1024]{2,1,0:T(1,128)} %constant.22.clone.mid_s) | copy-start | bytes 24580
  2.6 0.9 %copy-start.7 = (f32[2,1,512]{2,1,0:T(1,128)S(1)}, f32[2,1,512]{2,1,0:T(1,128)}, u32[]{:S(2)}) copy-start(f32[2,1,512]{2,1,0:T(1,128)} %constant.21.clone.cap_s) | copy-start | bytes 12292
  2.6 0.9 %copy-start.8 = (f32[2,388]{1,0:T(2,128)S(1)}, f32[2,388]{1,0:T(2,128)}, u32[]{:S(2)}) copy-start(f32[2,388]{1,0:T(2,128)} %constant.20.clone.rows_s) | copy-start | bytes 9316
  2.6 0.9 %copy-start.9 = (s32[2,384]{1,0:T(2,128)S(1)}, s32[2,384]{1,0:T(2,128)}, u32[]{:S(2)}) copy-start(s32[2,384]{1,0:T(2,128)} %cuts.1) | copy-start | bytes 9220
  2.6 0.9 %copy-start.10 = (f32[1,128]{1,0:T(1,128)S(1)}, f32[1,128]{1,0:T(1,128)}, u32[]{:S(2)}) copy-start(f32[1,128]{1,0:T(1,128)} %constant.29.clone.w_ref) | copy-start | bytes 1540

commit v3 on v2

v3 whole, which is shorter than its diff:
```python
import functools
import math

import jax
import jax.numpy as jnp
import ml_dtypes
import numpy as np
from jax import lax
from jax.experimental import pallas as pl
from jax.experimental.pallas import tpu as pltpu
from jax.sharding import PartitionSpec as P

MESH = pl.DeviceIdType.MESH
LEV, SEG, ROWS, SEGS = 4, 45, 1152, 128
CAP = ROWS // 3
CHUNK, WIN = 12, 16
PER = CAP // CHUNK
CW = 512
SHIFT = CW - CAP - 4
MW = 1024
KMAX = 128
C8 = 48
RET = 5
COLS = 101
TAIL = 7
F32, BF16 = jnp.float32, jnp.bfloat16


def split(x):
    hi = x.astype(ml_dtypes.bfloat16)
    return hi, (x - hi.astype(np.float32)).astype(ml_dtypes.bfloat16)


def two_parts(basis):
    hi, lo = split(np.ascontiguousarray(basis))
    return np.concatenate(
        [np.concatenate([hi, lo], axis=1), np.concatenate([hi, np.zeros_like(lo)], axis=1)], axis=0
    )


def tables():
    total = SEG * SEGS
    half = KMAX // 2
    m, s, c = np.arange(half), np.arange(SEGS), np.arange(SEG)
    a = 2 * np.pi * ((s[:, None] * m[None, :]) % SEGS) / SEGS
    sin = np.sin(a)
    sin[:, 0] = np.where(s % 2 == 0, 1.0, -1.0)
    basis = np.concatenate([np.cos(a), sin], axis=1).astype(np.float32)
    other = np.where(m == 0, half, KMAX - m)
    angle = lambda k: 2 * np.pi * (c[:, None] * k[None, :]) / total
    cm, sm, co, so = np.cos(angle(m)), np.sin(angle(m)), np.cos(angle(other)), np.sin(angle(other))
    ta, tb = np.concatenate([cm, -sm], axis=1), np.concatenate([sm, cm], axis=1)
    pa, pb = np.concatenate([co, so], axis=1), np.concatenate([so, -co], axis=1)
    ta[:, half], tb[:, half], pa[:, 0], pb[:, 0] = 0.0, 0.0, 0.0, 0.0
    pa[:, half], pb[:, half] = co[:, 0], so[:, 0]
    twiddle = np.pad(np.stack([ta, tb, pa, pb]), ((0, 0), (0, C8 - SEG), (0, 0))).astype(np.float32)
    return two_parts(basis), two_parts(basis.T), twiddle


def stretch_table():
    colat = np.float32(math.pi) * (np.arange(2 * ROWS).astype(np.float32) + np.float32(0.5))
    colat = (colat / np.float32(2 * ROWS)).astype(np.float32)
    s = np.float32(1.0) / np.maximum(np.sin(colat), np.float32(0.125))
    s = np.pad(s.astype(np.float32), (0, MW))
    cap = np.stack([s[:CW], s[2 * ROWS - CW : 2 * ROWS]])[:, None, :]
    mid = np.stack([s[256 : 256 + MW], s[ROWS - 128 : ROWS - 128 + MW]])[:, None, :]
    rows = np.stack([s[: CAP + 4], s[2 * ROWS - CAP - 4 : 2 * ROWS]])
    return cap, mid, rows


def tend(mid, east, west, north, south, u, v, s):
    return (
        -0.05 * s * u * (east - west)
        - 0.05 * v * (north - south)
        + 0.02 * s * (east - 2.0 * mid + west)
    )


def product(x, parts_ref):
    hi = x.astype(BF16)
    lo = (x - hi.astype(F32)).astype(BF16)
    r = jnp.dot(jnp.concatenate([hi, lo], axis=1), parts_ref[...], preferred_element_type=F32)
    return r[:, 0:128] + r[:, 128:]


def kernel(
    f_hbm, u_hbm, v_hbm, cuts, rows_s, cap_s, mid_s, fwd, inv, twiddle,
    out,
    f, u, v, mid_w, mid_e, mgot_w, mgot_e,
    fm, um, vm, mm, mx, ln, lx, msg, recv, ext, ext_got, sp,
    tt, uu, vv, ga, gb, st, ret, back, rl,
    cs, os, ms, mr, ls, lr, a_s, a_r, x_s, x_r, b_s, b_r,
):
    lat = lax.axis_index("lat")
    lon = lax.axis_index("lon")
    south = lat == 1
    jj = lax.rem(lon, PER)
    north_pole = jnp.logical_and(lat == 0, jj == 0)
    south_pole = jnp.logical_and(lat == 1, jj == PER - 1)
    at = lambda d: (lat, d)
    east_dev = at(lax.rem(lon + 1, SEGS))
    west_dev = at(lax.rem(lon + SEGS - 1, SEGS))
    partner = (1 - lat, lon)

    cap0 = pl.multiple_of(lat * (ROWS - CW), 128)
    mid0 = pl.multiple_of((1 - lat) * 256, 128)
    rest0 = pl.multiple_of((1 - lat) * CW, 128)
    pairs = ((f_hbm, f), (u_hbm, u), (v_hbm, v))

    caps = [
        pltpu.make_async_copy(src.at[:, :, pl.ds(cap0, CW)], dst.at[:, :, pl.ds(cap0, CW)], cs.at[i])
        for i, (src, dst) in enumerate(pairs)
    ]
    others = [
        pltpu.make_async_copy(
            src.at[:, :, pl.ds(rest0, ROWS - CW)], dst.at[:, :, pl.ds(rest0, ROWS - CW)], os.at[i]
        )
        for i, (src, dst) in enumerate(pairs)
    ]
    for c in caps:
        c.start()

    barrier = pltpu.get_barrier_semaphore()

    def greet(k):
        pl.semaphore_signal(barrier, inc=1, device_id=at(lax.rem(lon + k, SEGS)), device_id_type=MESH)

    @pl.loop(0, (SEGS - 1) // 8)
    def _(k):
        for i in range(8):
            greet(8 * k + i + 1)

    for k in range((SEGS - 1) // 8 * 8 + 1, SEGS):
        greet(k)
    pl.semaphore_signal(barrier, inc=1, device_id=partner, device_id_type=MESH)

    for c in others:
        c.start()

    lanes = lax.broadcasted_iota(jnp.int32, (C8, CW), 1)
    scap = cap_s[lat]
    row = lax.broadcasted_iota(jnp.int32, (WIN, 128), 0)
    lane1 = lanes[:SEG]
    pole = jnp.where(lat == 0, 0, CW - 1)

    for c in caps:
        c.wait()

    @pl.loop(0, LEV)
    def _(l):
        fc = f[l, :, pl.ds(cap0, CW)]
        uc = u[l, :, pl.ds(cap0, CW)]
        vc = v[l, :, pl.ds(cap0, CW)]
        zero = jnp.zeros((1, CW), F32)
        e = jnp.concatenate([fc[1:], zero], axis=0)
        w = jnp.concatenate([zero, fc[:-1]], axis=0)
        n = jnp.where(jnp.logical_and(lane1 == pole, lat == 0), 0.0, pltpu.roll(fc, 1, 1))
        s = jnp.where(jnp.logical_and(lane1 == pole, lat == 1), 0.0, pltpu.roll(fc, CW - 1, 1))
        turn = lax.rem(CW - lat * SHIFT, CW)
        mm[0:SEG] = pltpu.roll(tend(fc, e, w, n, s, uc, vc, scap), turn, 1)
        mm[SEG : 2 * SEG] = pltpu.roll(uc, turn, 1)
        mm[2 * SEG : 3 * SEG] = pltpu.roll(vc, turn, 1)
        vt = mm[128 : 128 + TAIL]
        x12 = lax.rem(lanes[:WIN], 12)
        edge = pltpu.roll(fc, lax.rem(CW - lat * (SHIFT + 2) + 1, CW), 1)
        mx[0:SEG] = jnp.where(lane1 == jnp.where(lat == 0, 1, CAP + 2), edge, mm[0:SEG])
        for i in range(8):
            t0 = i + 1 if i < 7 else 15
            t15 = i + 8 if i < 7 else 0
            a0 = pltpu.roll(vt, CW - t0, 1)
            a15 = pltpu.roll(vt, 15 - t15, 1)
            mx[SEG + TAIL * i : SEG + TAIL * (i + 1)] = jnp.where(x12[:TAIL] == 3, a15, a0)
        ft = pltpu.roll(fc, turn, 1)
        f0 = jnp.broadcast_to(ft[0:1], (WIN, CW))
        f44 = jnp.broadcast_to(ft[SEG - 1 : SEG], (WIN, CW))
        f0 = pltpu.roll(f0, CW - 15, 1, stride=1, stride_axis=0)
        f44 = pltpu.roll(f44, 0, 1, stride=1, stride_axis=0)
        mx[COLS : COLS + WIN] = jnp.where(x12 == 3, f44, f0)
        mx[COLS + WIN : COLS + WIN + 1] = mm[SEG : SEG + 1]
        mx[COLS + WIN + 1 : COLS + WIN + 2] = mm[2 * SEG - 1 : 2 * SEG]
        for b in range(CW // 128):
            ln[128 * b : 128 * (b + 1)] = mm[0:128, 128 * b : 128 * (b + 1)].T
            lx[128 * b : 128 * (b + 1)] = mx[0:128, 128 * b : 128 * (b + 1)].T

        @pl.loop(0, PER // 8)
        def _(mo):
            for mi in range(4):
                m = 4 * mo + mi
                a = ln[pl.ds(pl.multiple_of(24 * m, 8), 32)]
                b = lx[pl.ds(pl.multiple_of(24 * m, 8), 32)]
                first = jnp.logical_and(m == 0, lat == 0)
                last = jnp.logical_and(m == PER // 2 - 1, lat == 1)
                use0 = jnp.logical_or(jnp.logical_and(row == 0, jnp.logical_not(first)), row == WIN - 1)
                use1 = jnp.logical_or(row == 0, jnp.logical_and(row == WIN - 1, jnp.logical_not(last)))
                msg[l * PER + 2 * m] = jnp.where(use0, b[0:16], a[0:16])
                msg[l * PER + 2 * m + 1] = jnp.where(use1, b[12:28], a[12:28])

        ext[l] = jnp.where(lat == 0, lx[0:8], lx[CAP - 4 : CAP + 4])

    pl.semaphore_wait(barrier, SEGS)

    def remote(src, dst, send, recv_sem, dev):
        return pltpu.make_async_remote_copy(
            src_ref=src, dst_ref=dst, send_sem=send, recv_sem=recv_sem,
            device_id=dev, device_id_type=MESH,
        )

    def send_line(d):
        return remote(msg.at[d], recv.at[lon], a_s, a_r, at(d))

    def spread(send):
        @pl.loop(0, (SEGS // 2 - 1) // 7)
        def _(k):
            for i in range(1, 8):
                send(lax.rem(lon + 7 * k + i, SEGS)).start()
                send(lax.rem(lon + SEGS - 7 * k - i, SEGS)).start()

        send(lax.rem(lon + SEGS // 2, SEGS)).start()

    spread(send_line)
    recv[lon] = msg[lon]

    def send_ext(l):
        d = l * PER + lat * (PER - 1)
        return d, remote(ext.at[l], ext_got.at[lon], x_s.at[l], x_r, at(d))

    for l in range(LEV):
        d, c = send_ext(l)

        @pl.when(d != lon)
        def _():
            c.start()

        @pl.when(d == lon)
        def _():
            ext_got[lon] = ext[l]

    for c in others:
        c.wait()
    own = pl.multiple_of(lat * 128, 128)
    mid_w[...] = jnp.zeros_like(mid_w)
    mid_e[...] = jnp.zeros_like(mid_e)
    parts = ((fm, f, 0, 3), (um, u, 3, 2), (vm, v, 5, 2))
    for l in range(LEV):
        for ref, src, a, n in parts:
            mid_w[l, a : a + n] = src[l, 0:n, pl.ds(mid0, MW - 128)]
            mid_e[l, a : a + n] = src[l, SEG - n : SEG, pl.ds(mid0, MW - 128)]

    @pl.loop(0, LEV)
    def _(l):
        for ref, src, a, n in parts:
            ref[l, 3 : 3 + SEG, pl.ds(own, MW - 128)] = src[l, :, pl.ds(mid0, MW - 128)]

    mids = [
        remote(mid_w, mgot_e, ms.at[0], mr.at[0], west_dev),
        remote(mid_e, mgot_w, ms.at[1], mr.at[1], east_dev),
    ]
    src0 = pl.multiple_of((1 - lat) * (MW - 256) + lat * 128, 128)
    dst0 = pl.multiple_of(lat * (MW - 128), 128)
    lats = [
        remote(ref.at[:, :, pl.ds(src0, 128)], ref.at[:, :, pl.ds(dst0, 128)], ls.at[i], lr.at[i], partner)
        for i, ref in enumerate((fm, um, vm))
    ]

    def total(sem, ref, n):
        pltpu.make_async_copy(ref.at[pl.ds(0, n)], ref.at[pl.ds(0, n)], sem).wait()

    total(a_r, recv, SEGS - 1)
    for c in mids:
        c.start()
    tt[:, SEG:C8] = jnp.zeros((WIN, C8 - SEG, 128), F32)
    uu[:, SEG:C8] = jnp.zeros((WIN, C8 - SEG, 128), F32)
    vv[:, SEG:C8] = jnp.zeros((WIN, C8 - SEG, 128), F32)
    for t in range(WIN):
        w = recv[:, t, :].T
        tt[t, 0:SEG] = w[0:SEG]
        uu[t, 0:SEG] = w[SEG : 2 * SEG]
        vv[t, 0 : SEG - TAIL] = w[2 * SEG : 128]
        if t == 0:
            sp[0] = w
        if t == WIN - 1:
            sp[1] = w

    @pl.when(jnp.logical_or(north_pole, south_pole))
    def _():
        total(x_r, ext_got, SEGS - 1)

    sp[2] = jnp.zeros((128, 128), F32)

    @pl.when(north_pole)
    def _():
        sp[0] = ext_got[:, 0, :].T
        sp[2] = ext_got[:, 1, :].T

    @pl.when(south_pole)
    def _():
        sp[1] = ext_got[:, 7, :].T
        sp[2] = ext_got[:, 6, :].T

    for i in range(8):
        t0 = i + 1 if i < 7 else 15
        t15 = i + 8 if i < 7 else 0
        lo, hi = SEG + TAIL * i, SEG + TAIL * (i + 1)
        vv[t0, SEG - TAIL : SEG] = sp[0, lo:hi]
        vv[t15, SEG - TAIL : SEG] = sp[1, lo:hi]

    e_in = pltpu.roll(sp[0, COLS - 5 : COLS + 19], 127, 1)
    w_in = pltpu.roll(sp[1, COLS - 5 : COLS + 19], 1, 1)
    for t in range(WIN):
        sw = rows_s[lat, CHUNK * jj + t]
        if t in (0, WIN - 1):
            u0 = sp[t // (WIN - 1), COLS + WIN : COLS + WIN + 1]
            u44 = sp[t // (WIN - 1), COLS + WIN + 1 : COLS + WIN + 2]
        else:
            u0, u44 = uu[t, 0:1], uu[t, SEG - 1 : SEG]
        r = 5 + 15 - t
        tt[t, SEG - 1 : SEG] += (0.02 * sw - 0.05 * sw * u44) * e_in[r : r + 1]
        tt[t, 0:1] += (0.02 * sw + 0.05 * sw * u0) * w_in[r : r + 1]
    opp = 0.05 * pltpu.roll(sp[2, 0:C8], SEGS // 2, 1)[:SEG]
    tt[0, 0:SEG] -= jnp.where(north_pole, vv[0, 0:SEG] * opp, 0.0)
    tt[WIN - 1, 0:SEG] += jnp.where(south_pole, vv[WIN - 1, 0:SEG] * opp, 0.0)

    col = lax.broadcasted_iota(jnp.int32, (C8, 128), 0)
    m_lane = lax.rem(lax.broadcasted_iota(jnp.int32, (1, KMAX), 1), KMAX // 2)
    o_lane = jnp.where(m_lane == 0, KMAX // 2, KMAX - m_lane)
    w_m = jnp.where(m_lane == 0, 1.0 / (SEG * SEGS), 2.0 / (SEG * SEGS))
    w_o = 2.0 / (SEG * SEGS)

    def lap(old, t):
        g = old[t]
        g8 = pltpu.roll(g[0:8], 127, 1)
        g40 = pltpu.roll(g[40:48], 1, 1)
        e = jnp.where(col == SEG - 1, jnp.broadcast_to(g8[0:1], (C8, 128)), pltpu.roll(g, C8 - 1, 0))
        w = jnp.where(col == 0, jnp.broadcast_to(g40[4:5], (C8, 128)), pltpu.roll(g, 1, 0))
        n = old[max(t - 1, 0)]
        s = old[min(t + 1, WIN - 1)]
        if t == 0:
            n = jnp.where(north_pole, pltpu.roll(g, SEGS // 2, 1), n)
        if t == WIN - 1:
            s = jnp.where(south_pole, pltpu.roll(g, SEGS // 2, 1), s)
        return tend(g, e, w, n, s, uu[t], vv[t], rows_s[lat, CHUNK * jj + t])

    def fold(z, table):
        p = jnp.sum(z * table, axis=0, keepdims=True)
        return p + pltpu.roll(p, KMAX // 2, 1)

    def substep(step, old, new, block):
        ts = range(4 * block, 4 * block + 4)
        raw = [tt[t] if step == 0 else tt[t] + lap(old, t) for t in ts]
        z = product(jnp.concatenate(raw, axis=0), fwd)
        modes = []
        for i, t in enumerate(ts):
            zt = z[C8 * i : C8 * (i + 1)]
            x = CHUNK * jj + t - 4 * lat
            cut = cuts[lat, jnp.minimum(jnp.maximum(x, 0), CAP - 1)]
            km = jnp.where(m_lane <= cut, w_m, 0.0)
            ko = jnp.where(o_lane <= cut, w_o, 0.0)
            modes.append(
                (fold(zt, twiddle[0]) * km) * twiddle[0]
                + (fold(zt, twiddle[1]) * km) * twiddle[1]
                + (fold(zt, twiddle[2]) * ko) * twiddle[2]
                + (fold(zt, twiddle[3]) * ko) * twiddle[3]
            )
        y = product(jnp.concatenate(modes, axis=0), inv)
        for i, t in enumerate(ts):
            x = CHUNK * jj + t - 4 * lat
            inside = jnp.logical_and(x >= 0, x < CAP)
            g = jnp.where(inside, y[C8 * i : C8 * (i + 1)], raw[i])
            new[t] = g if step == 0 else old[t] + g

    for step, (old, new) in enumerate(((gb, ga), (ga, gb), (gb, ga))):
        for block in range(WIN // 4):
            substep(step, old, new, block)
        if step == 0:
            for c in mids:
                c.wait()
            for l in range(LEV):
                for ref, src, a, n in parts:
                    ref[l, 3 - n : 3, pl.ds(own, MW - 128)] = mgot_w[l, a : a + n]
                    ref[l, 3 + SEG : 3 + SEG + n, pl.ds(own, MW - 128)] = mgot_e[l, a : a + n]
            for c in lats:
                c.start()

    for i in range(CHUNK):
        st[SEG * i : SEG * (i + 1)] = ga[2 + i, 0:SEG]
    for i in range(2):
        st[SEG * (CHUNK + i) : SEG * (CHUNK + i + 1)] = jnp.where(lat == 0, ga[i, 0:SEG], ga[WIN - 2 + i, 0:SEG])
    st[SEG * (CHUNK + 2) :] = jnp.zeros((128 * RET - SEG * (CHUNK + 2), 128), F32)
    for p in range(RET):
        ret[:, p, :] = st[128 * p : 128 * (p + 1)].T

    def send_back(d):
        return remote(ret.at[d], back.at[lon], b_s, b_r, at(d))

    spread(send_back)
    back[lon] = ret[lon]

    for c in lats:
        c.wait()
    smid = mid_s[lat]

    @pl.loop(0, LEV)
    def _(l):
        for _ in range(3):
            x = fm[l]
            t = tend(
                x, pltpu.roll(x, 55, 0), pltpu.roll(x, 1, 0),
                pltpu.roll(x, 1, 1), pltpu.roll(x, MW - 1, 1), um[l], vm[l], smid,
            )
            fm[l] = x + t

    @pl.loop(0, LEV)
    def _(l):
        out[l, :, pl.ds(mid0, MW - 128)] = fm[l, 3 : 3 + SEG, pl.ds(own, MW - 128)]

    total(b_r, back, SEGS - 1)
    rl[:, CAP:CW] = jnp.zeros((LEV, CW - CAP, 128), F32)
    lane128 = lax.broadcasted_iota(jnp.int32, (SEGS, 128), 1)
    for i in range(CHUNK + 2):
        p, off = divmod(SEG * i, 128)
        r = back[:, p, :]
        if off:
            r = pltpu.roll(r, 128 - off, 1)
        if off + SEG > 128:
            r = jnp.where(lane128 < 128 - off, r, pltpu.roll(back[:, p + 1, :], 128 - off, 1))
        for l in range(LEV):
            if i < CHUNK:
                rl[l, pl.ds(2 + i, PER, stride=CHUNK), :] = r[PER * l : PER * (l + 1)]
            else:
                rl[l, i - CHUNK : i - CHUNK + 1] = r[PER * l : PER * l + 1]
                rl[l, CAP + 2 + i - CHUNK : CAP + 3 + i - CHUNK] = r[PER * (l + 1) - 1 : PER * (l + 1)]

    for l in range(LEV):
        add = jnp.concatenate([rl[l, 128 * b : 128 * (b + 1)].T[0:C8] for b in range(CW // 128)], axis=1)
        add = pltpu.roll(add, lat * SHIFT, 1)[0:SEG]
        x = lane1 - lat * SHIFT
        inside = jnp.logical_and(x >= 2 * lat, x < CAP + 2 + 2 * lat)
        old = out[l, :, pl.ds(cap0, CW)]
        out[l, :, pl.ds(cap0, CW)] = jnp.where(inside, f[l, :, pl.ds(cap0, CW)] + add, old)

    total(a_s, msg, SEGS - 1)
    total(b_s, ret, SEGS - 1)
    for l in range(LEV):
        d, c = send_ext(l)

        @pl.when(d != lon)
        def _():
            c.wait_send()


def body(f, u, v, cutoffs):
    cap_s, mid_s, rows_s = stretch_table()
    vmem = pl.BlockSpec(memory_space=pltpu.VMEM)
    smem = pl.BlockSpec(memory_space=pltpu.SMEM)
    V = lambda *shape: pltpu.VMEM(shape, F32)
    dma = pltpu.SemaphoreType.DMA
    return pl.pallas_call(
        kernel,
        out_shape=jax.ShapeDtypeStruct(f.shape, F32),
        in_specs=[pl.BlockSpec(memory_space=pl.ANY)] * 3 + [smem] * 2 + [vmem] * 5,
        out_specs=vmem,
        scratch_shapes=[
            V(LEV, SEG, ROWS), V(LEV, SEG, ROWS), V(LEV, SEG, ROWS),
            V(LEV, 8, MW - 128), V(LEV, 8, MW - 128), V(LEV, 8, MW - 128), V(LEV, 8, MW - 128),
            V(LEV, 56, MW), V(LEV, 56, MW), V(LEV, 56, MW),
            V(136, CW), V(128, CW), V(CW, 128), V(CW, 128),
            V(SEGS, WIN, 128), V(SEGS, WIN, 128), V(LEV, 8, 128), V(SEGS, 8, 128), V(3, 128, 128),
            V(WIN, C8, 128), V(WIN, C8, 128), V(WIN, C8, 128), V(WIN, C8, 128), V(WIN, C8, 128),
            V(128 * RET, 128), V(SEGS, RET, 128), V(SEGS, RET, 128), V(LEV, CW, 128),
            dma((3,)), dma((3,)), dma((2,)), dma((2,)), dma((3,)), dma((3,)),
            dma, dma, dma((LEV,)), dma, dma, dma,
        ],
        compiler_params=pltpu.CompilerParams(
            collective_id=0, has_side_effects=True, vmem_limit_bytes=40 * 1024 * 1024
        ),
    )(f, u, v, cutoffs, rows_s, cap_s, mid_s, *tables())


def solution(mesh):
    placed = (P(None, "lon", "lat"), P(None, "lon", "lat"), P(None, "lon", "lat"), P())
    return jax.shard_map(
        body, mesh=mesh, in_specs=placed, out_specs=P(None, "lon", "lat"), check_vma=False
    )
```

time: 80 us -> 62.9 us (0.79)
  Pallas kernels: 74.3 us -> 57.7 us
    pallas_call x1, Pallas kernels: 74.3 us -> 57.7 us  [body(): pl.pallas_call(kernel, out_shape=jax.ShapeDtypeStruct(f.shape, F32), in_s...]
    unnamed x29 -> x21, local copies, waits for them, and re-layouts: 3.42 us -> 3.53 us
where the time goes in v3:
time: 62.9 us; the launch traced here: 62.5 us
  Pallas kernels  57.7 us (92%)
  local copies, waits for them, and re-layouts  4.74 us (8%)
    pallas_call x1, Pallas kernels, body(): pl.pallas_call(kernel, out_shape=jax.ShapeDtypeStruct(f.shape, F32), in_s...  57.7 us
    unnamed x21, local copies, waits for them, and re-layouts  3.53 us

profile of v3, /device:TPU:8, one launch (start us, length us, event | category | flops | bytes accessed | tf_op | source)
XLA Modules:
  0.0 62.5 jit_solution(5002921007217581569)
XLA Ops:
  0.0 0.0 copy-start.7
  0.0 1.3 %copy.11.f_hbm = f32[4,45,1152]{2,1,0:T(8,128)S(1)} copy(f32[4,45,1152]{2,0,1:T(4,128)} %param.10) | data formatting | bytes 1658880 | tf_op args[0]
  1.3 0.1 copy-done.7
  1.4 0.0 copy-start.8
  1.4 0.1 copy.12.u_hbm
  1.5 1.1 %copy-done.8 = f32[4,45,1152]{2,0,1:T(4,128)S(1)} copy-done((f32[4,45,1152]{2,0,1:T(4,128)S(1)}, f32[4,45,1152]{2,0,1:T(4,128)}, u32[]{:S(2)}) %copy-start.8) | copy-done | bytes 829464
  2.5 0.0 copy-start
  2.5 0.0 copy-start.1
  2.6 0.0 copy-start.2
  2.6 0.0 copy-start.3
  2.6 0.0 copy-start.4
  2.6 0.0 copy-start.5
  2.6 0.0 copy-start.6
  2.6 0.1 copy.13.v_hbm
  2.7 0.8 %copy-done = bf16[256,256]{1,0:T(8,128)(2,1)S(1)} copy-done((bf16[256,256]{1,0:T(8,128)(2,1)S(1)}, bf16[256,256]{1,0:T(8,128)(2,1)}, u32[]{:S(2)}) %copy-start) | copy-done | bytes 131096
  3.5 0.1 copy-done.1
  3.5 0.1 copy-done.2
  3.6 0.0 copy-done.3
  3.6 0.0 copy-done.4
  3.6 0.0 copy-done.5
  3.6 0.0 copy-done.6
  3.6 57.7 %shard_map.100 = f32[4,45,1152]{2,1,0:T(8,128)S(1)} custom-call(f32[4,45,1152]{2,1,0:T(8,128)S(1)} %copy.11.f_hbm, f32[4,45,1152]{2,1,0:T(8,128)S(1)} %copy.12.u_hbm, f32[4,45,1152]{2,1,0:T(8,128)S(1)} %copy.13.v_hbm, s32[2,384]{1,0:T(2,128)S(1)} %copy-done.6, f32[2,388]{1,0:T(2,128)S(1)} %copy-done.5, f32[2,1,512]{2,1,0:T(1,128)S(1)} %copy-done.4, ...), custom_call_target="tpu_custom_call" | custom-call | tf_op jit(solution)/shard_map/pallas_call | solution.py:457
  61.3 1.2 %copy.14 = f32[4,45,1152]{2,0,1:T(4,128)} copy(f32[4,45,1152]{2,1,0:T(8,128)S(1)} %shard_map.100) | data formatting | bytes 1658880 | tf_op jit(solution)/shard_map/pallas_call | solution.py:457
Async XLA Ops:
  0.0 1.4 %copy-start.7 = (f32[4,45,1152]{2,0,1:T(4,128)S(1)}, f32[4,45,1152]{2,0,1:T(4,128)}, u32[]{:S(2)}) copy-start(f32[4,45,1152]{2,0,1:T(4,128)} %param.11) | copy-start | bytes 2488324
  1.4 1.1 %copy-start.8 = (f32[4,45,1152]{2,0,1:T(4,128)S(1)}, f32[4,45,1152]{2,0,1:T(4,128)}, u32[]{:S(2)}) copy-start(f32[4,45,1152]{2,0,1:T(4,128)} %param.12) | copy-start | bytes 2488324
  2.5 0.9 %copy-start = (bf16[256,256]{1,0:T(8,128)(2,1)S(1)}, bf16[256,256]{1,0:T(8,128)(2,1)}, u32[]{:S(2)}) copy-start(bf16[256,256]{1,0:T(8,128)(2,1)} %constant.16.clone.inv) | copy-start | bytes 393220
  2.5 1.0 %copy-start.1 = (bf16[256,256]{1,0:T(8,128)(2,1)S(1)}, bf16[256,256]{1,0:T(8,128)(2,1)}, u32[]{:S(2)}) copy-start(bf16[256,256]{1,0:T(8,128)(2,1)} %constant.15.clone.fwd) | copy-start | bytes 393220
  2.6 1.0 %copy-start.2 = (f32[4,48,128]{2,1,0:T(8,128)S(1)}, f32[4,48,128]{2,1,0:T(8,128)}, u32[]{:S(2)}) copy-start(f32[4,48,128]{2,1,0:T(8,128)} %constant.17.clone.twiddle) | copy-start | bytes 294916
  2.6 1.0 %copy-start.3 = (f32[2,1,1024]{2,1,0:T(1,128)S(1)}, f32[2,1,1024]{2,1,0:T(1,128)}, u32[]{:S(2)}) copy-start(f32[2,1,1024]{2,1,0:T(1,128)} %constant.14.clone.mid_s) | copy-start | bytes 24580
  2.6 1.0 %copy-start.4 = (f32[2,1,512]{2,1,0:T(1,128)S(1)}, f32[2,1,512]{2,1,0:T(1,128)}, u32[]{:S(2)}) copy-start(f32[2,1,512]{2,1,0:T(1,128)} %constant.13.clone.cap_s) | copy-start | bytes 12292
  2.6 1.0 %copy-start.5 = (f32[2,388]{1,0:T(2,128)S(1)}, f32[2,388]{1,0:T(2,128)}, u32[]{:S(2)}) copy-start(f32[2,388]{1,0:T(2,128)} %constant.12.clone.rows_s) | copy-start | bytes 9316
  2.6 1.0 %copy-start.6 = (s32[2,384]{1,0:T(2,128)S(1)}, s32[2,384]{1,0:T(2,128)}, u32[]{:S(2)}) copy-start(s32[2,384]{1,0:T(2,128)} %cuts.1) | copy-start | bytes 9220

commit v4 on v3

--- a/solution.py
+++ b/solution.py
@@ -85,11 +85,11 @@
 
 def kernel(
     f_hbm, u_hbm, v_hbm, cuts, rows_s, cap_s, mid_s, fwd, inv, twiddle,
-    out,
-    f, u, v, mid_w, mid_e, mgot_w, mgot_e,
+    out_hbm,
+    out, f, u, v, mid_w, mid_e, mgot_w, mgot_e,
     fm, um, vm, mm, mx, ln, lx, msg, recv, ext, ext_got, sp,
     tt, uu, vv, ga, gb, st, ret, back, rl,
-    cs, os, ms, mr, ls, lr, a_s, a_r, x_s, x_r, b_s, b_r,
+    d_s, cs, os, ms, mr, ls, lr, a_s, a_r, x_s, x_r, b_s, b_r,
 ):
     lat = lax.axis_index("lat")
     lon = lax.axis_index("lon")
@@ -107,18 +107,16 @@
     rest0 = pl.multiple_of((1 - lat) * CW, 128)
     pairs = ((f_hbm, f), (u_hbm, u), (v_hbm, v))
 
-    caps = [
-        pltpu.make_async_copy(src.at[:, :, pl.ds(cap0, CW)], dst.at[:, :, pl.ds(cap0, CW)], cs.at[i])
-        for i, (src, dst) in enumerate(pairs)
-    ]
-    others = [
-        pltpu.make_async_copy(
-            src.at[:, :, pl.ds(rest0, ROWS - CW)], dst.at[:, :, pl.ds(rest0, ROWS - CW)], os.at[i]
+    def load(i, l, first, lanes, sems):
+        src, dst = pairs[i]
+        return pltpu.make_async_copy(
+            src.at[:, l, pl.ds(first, lanes)], dst.at[l, :, pl.ds(first, lanes)], sems.at[i, l]
         )
-        for i, (src, dst) in enumerate(pairs)
-    ]
-    for c in caps:
-        c.start()
+
+    others = [load(i, l, rest0, ROWS - CW, os) for l in range(LEV) for i in range(3)]
+    for l in range(LEV):
+        for i in range(3):
+            load(i, l, cap0, CW, cs).start()
 
     barrier = pltpu.get_barrier_semaphore()
 
@@ -143,11 +141,10 @@
     lane1 = lanes[:SEG]
     pole = jnp.where(lat == 0, 0, CW - 1)
 
-    for c in caps:
-        c.wait()
-
     @pl.loop(0, LEV)
     def _(l):
+        for i in range(3):
+            load(i, l, cap0, CW, cs).wait()
         fc = f[l, :, pl.ds(cap0, CW)]
         uc = u[l, :, pl.ds(cap0, CW)]
         vc = v[l, :, pl.ds(cap0, CW)]
@@ -265,9 +262,10 @@
     def total(sem, ref, n):
         pltpu.make_async_copy(ref.at[pl.ds(0, n)], ref.at[pl.ds(0, n)], sem).wait()
 
-    total(a_r, recv, SEGS - 1)
+    total(a_s, msg, SEGS - 1)
     for c in mids:
         c.start()
+    total(a_r, recv, SEGS - 1)
     tt[:, SEG:C8] = jnp.zeros((WIN, C8 - SEG, 128), F32)
     uu[:, SEG:C8] = jnp.zeros((WIN, C8 - SEG, 128), F32)
     vv[:, SEG:C8] = jnp.zeros((WIN, C8 - SEG, 128), F32)
@@ -371,15 +369,6 @@
     for step, (old, new) in enumerate(((gb, ga), (ga, gb), (gb, ga))):
         for block in range(WIN // 4):
             substep(step, old, new, block)
-        if step == 0:
-            for c in mids:
-                c.wait()
-            for l in range(LEV):
-                for ref, src, a, n in parts:
-                    ref[l, 3 - n : 3, pl.ds(own, MW - 128)] = mgot_w[l, a : a + n]
-                    ref[l, 3 + SEG : 3 + SEG + n, pl.ds(own, MW - 128)] = mgot_e[l, a : a + n]
-            for c in lats:
-                c.start()
 
     for i in range(CHUNK):
         st[SEG * i : SEG * (i + 1)] = ga[2 + i, 0:SEG]
@@ -394,6 +383,14 @@
 
     spread(send_back)
     back[lon] = ret[lon]
+    for c in mids:
+        c.wait()
+    for l in range(LEV):
+        for ref, src, a, n in parts:
+            ref[l, 3 - n : 3, pl.ds(own, MW - 128)] = mgot_w[l, a : a + n]
+            ref[l, 3 + SEG : 3 + SEG + n, pl.ds(own, MW - 128)] = mgot_e[l, a : a + n]
+    for c in lats:
+        c.start()
 
     for c in lats:
         c.wait()
@@ -430,6 +427,7 @@
                 rl[l, i - CHUNK : i - CHUNK + 1] = r[PER * l : PER * l + 1]
                 rl[l, CAP + 2 + i - CHUNK : CAP + 3 + i - CHUNK] = r[PER * (l + 1) - 1 : PER * (l + 1)]
 
+    stores = [pltpu.make_async_copy(out.at[l], out_hbm.at[:, l, :], d_s.at[l]) for l in range(LEV)]
     for l in range(LEV):
         add = jnp.concatenate([rl[l, 128 * b : 128 * (b + 1)].T[0:C8] for b in range(CW // 128)], axis=1)
         add = pltpu.roll(add, lat * SHIFT, 1)[0:SEG]
@@ -437,8 +435,8 @@
         inside = jnp.logical_and(x >= 2 * lat, x < CAP + 2 + 2 * lat)
         old = out[l, :, pl.ds(cap0, CW)]
         out[l, :, pl.ds(cap0, CW)] = jnp.where(inside, f[l, :, pl.ds(cap0, CW)] + add, old)
-
-    total(a_s, msg, SEGS - 1)
+        stores[l].start()
+
     total(b_s, ret, SEGS - 1)
     for l in range(LEV):
         d, c = send_ext(l)
@@ -446,6 +444,9 @@
         @pl.when(d != lon)
         def _():
             c.wait_send()
+
+    for c in stores:
+        c.wait()
 
 
 def body(f, u, v, cutoffs):
@@ -454,26 +455,28 @@
     smem = pl.BlockSpec(memory_space=pltpu.SMEM)
     V = lambda *shape: pltpu.VMEM(shape, F32)
     dma = pltpu.SemaphoreType.DMA
-    return pl.pallas_call(
+    f, u, v = (jnp.transpose(a, (1, 0, 2)) for a in (f, u, v))
+    done = pl.pallas_call(
         kernel,
         out_shape=jax.ShapeDtypeStruct(f.shape, F32),
         in_specs=[pl.BlockSpec(memory_space=pl.ANY)] * 3 + [smem] * 2 + [vmem] * 5,
-        out_specs=vmem,
+        out_specs=pl.BlockSpec(memory_space=pl.ANY),
         scratch_shapes=[
-            V(LEV, SEG, ROWS), V(LEV, SEG, ROWS), V(LEV, SEG, ROWS),
+            V(LEV, SEG, ROWS), V(LEV, SEG, ROWS), V(LEV, SEG, ROWS), V(LEV, SEG, ROWS),
             V(LEV, 8, MW - 128), V(LEV, 8, MW - 128), V(LEV, 8, MW - 128), V(LEV, 8, MW - 128),
             V(LEV, 56, MW), V(LEV, 56, MW), V(LEV, 56, MW),
             V(136, CW), V(128, CW), V(CW, 128), V(CW, 128),
             V(SEGS, WIN, 128), V(SEGS, WIN, 128), V(LEV, 8, 128), V(SEGS, 8, 128), V(3, 128, 128),
             V(WIN, C8, 128), V(WIN, C8, 128), V(WIN, C8, 128), V(WIN, C8, 128), V(WIN, C8, 128),
             V(128 * RET, 128), V(SEGS, RET, 128), V(SEGS, RET, 128), V(LEV, CW, 128),
-            dma((3,)), dma((3,)), dma((2,)), dma((2,)), dma((3,)), dma((3,)),
+            dma((LEV,)), dma((3, LEV)), dma((3, LEV)), dma((2,)), dma((2,)), dma((3,)), dma((3,)),
             dma, dma, dma((LEV,)), dma, dma, dma,
         ],
         compiler_params=pltpu.CompilerParams(
-            collective_id=0, has_side_effects=True, vmem_limit_bytes=40 * 1024 * 1024
+            collective_id=0, has_side_effects=True, vmem_limit_bytes=60 * 1024 * 1024
         ),
     )(f, u, v, cutoffs, rows_s, cap_s, mid_s, *tables())
+    return jnp.transpose(done, (1, 0, 2))
 
 
 def solution(mesh):

time: 62.9 us -> 58.1 us (0.924)
  local copies, waits for them, and re-layouts: 4.74 us -> 2.11 us
  Pallas kernels: 57.7 us -> 55.6 us
    pallas_call x1, Pallas kernels: 57.7 us -> 55.6 us  [body(): pl.pallas_call(kernel, out_shape=jax.ShapeDtypeStruct(f.shape, F32), in_s...]
    unnamed x21 -> x1, local copies, waits for them, and re-layouts: 3.53 us -> 2.11 us
    pallas_call x1 -> x0, local copies, waits for them, and re-layouts: 1.21 us -> none  [body(): pl.pallas_call(kernel, out_shape=jax.ShapeDtypeStruct(f.shape, F32), in_s...]
where the time goes in v4:
time: 58.1 us; the launch traced here: 57.7 us
  Pallas kernels  55.6 us (96%)
  local copies, waits for them, and re-layouts  2.11 us (4%)
    pallas_call x1, Pallas kernels, body(): pl.pallas_call(kernel, out_shape=jax.ShapeDtypeStruct(f.shape, F32), in_s...  55.6 us
    unnamed x1, local copies, waits for them, and re-layouts  2.11 us

profile of v4, /device:TPU:8, one launch (start us, length us, event | category | flops | bytes accessed | tf_op | source)
XLA Modules:
  0.0 57.7 jit_solution(14141504942100617190)
XLA Ops:
  0.0 55.6 %shard_map.100 = f32[45,4,1152]{2,1,0:T(4,128)} custom-call(f32[45,4,1152]{2,1,0:T(4,128)} %bitcast.5, f32[45,4,1152]{2,1,0:T(4,128)} %bitcast.6, f32[45,4,1152]{2,1,0:T(4,128)} %bitcast.7, s32[2,384]{1,0:T(2,128)} %cuts.1, f32[2,388]{1,0:T(2,128)} %constant.12.clone.rows_s, f32[2,1,512]{2,1,0:T(1,128)} %constant.13.clone.cap_s, ...), custom_call_target="tpu_custom_call" | custom-call | tf_op jit(solution)/shard_map/pallas_call | solution.py:459
  55.6 2.1 %copy.12 = f32[4,45,1152]{2,0,1:T(4,128)} copy(f32[4,45,1152]{2,0,1:T(4,128)} %bitcast.4) | data formatting | bytes 1658880

commit v5 on v4

--- a/solution.py
+++ b/solution.py
@@ -20,7 +20,9 @@
 MW = 1024
 KMAX = 128
 C8 = 48
+BLOCK = 16
 RET = 5
+SMALL = 7
 COLS = 101
 TAIL = 7
 F32, BF16 = jnp.float32, jnp.bfloat16
@@ -84,8 +86,15 @@
 
 
 def kernel(
-    f_hbm, u_hbm, v_hbm, cuts, rows_s, cap_s, mid_s, fwd, inv, twiddle,
-    out_hbm,
+    f_hbm, u_hbm, v_hbm, *rest,
+):
+    small, (out_hbm, *scratch) = rest[:SMALL], rest[SMALL:]
+    run(f_hbm, u_hbm, v_hbm, small, out_hbm, *scratch)
+
+
+def run(
+    f_hbm, u_hbm, v_hbm, small, out_hbm,
+    cuts, rows_s, cap_s, mid_s, fwd, inv, twiddle, small_s,
     out, f, u, v, mid_w, mid_e, mgot_w, mgot_e,
     fm, um, vm, mm, mx, ln, lx, msg, recv, ext, ext_got, sp,
     tt, uu, vv, ga, gb, st, ret, back, rl,
@@ -114,10 +123,6 @@
         )
 
     others = [load(i, l, rest0, ROWS - CW, os) for l in range(LEV) for i in range(3)]
-    for l in range(LEV):
-        for i in range(3):
-            load(i, l, cap0, CW, cs).start()
-
     barrier = pltpu.get_barrier_semaphore()
 
     def greet(k):
@@ -132,8 +137,19 @@
         greet(k)
     pl.semaphore_signal(barrier, inc=1, device_id=partner, device_id_type=MESH)
 
+    held = (cuts, rows_s, cap_s, mid_s, fwd, inv, twiddle)
+    smalls = [pltpu.make_async_copy(src, dst, small_s.at[i]) for i, (src, dst) in enumerate(zip(small, held))]
+    for l in range(LEV):
+        for i in range(3):
+            load(i, l, cap0, CW, cs).start()
+        if l == 0:
+            smalls[2].start()
+    for i, c in enumerate(smalls):
+        if i != 2:
+            c.start()
     for c in others:
         c.start()
+    smalls[2].wait()
 
     lanes = lax.broadcasted_iota(jnp.int32, (C8, CW), 1)
     scap = cap_s[lat]
@@ -192,7 +208,7 @@
                 msg[l * PER + 2 * m] = jnp.where(use0, b[0:16], a[0:16])
                 msg[l * PER + 2 * m + 1] = jnp.where(use1, b[12:28], a[12:28])
 
-        ext[l] = jnp.where(lat == 0, lx[0:8], lx[CAP - 4 : CAP + 4])
+        ext[l] = jnp.where(lat == 0, lx[0:2], lx[CAP + 2 : CAP + 4])
 
     pl.semaphore_wait(barrier, SEGS)
 
@@ -234,6 +250,9 @@
 
     for c in others:
         c.wait()
+    for i, c in enumerate(smalls):
+        if i != 2:
+            c.wait()
     own = pl.multiple_of(lat * 128, 128)
     mid_w[...] = jnp.zeros_like(mid_w)
     mid_e[...] = jnp.zeros_like(mid_e)
@@ -292,8 +311,8 @@
 
     @pl.when(south_pole)
     def _():
-        sp[1] = ext_got[:, 7, :].T
-        sp[2] = ext_got[:, 6, :].T
+        sp[1] = ext_got[:, 1, :].T
+        sp[2] = ext_got[:, 0, :].T
 
     for i in range(8):
         t0 = i + 1 if i < 7 else 15
@@ -343,7 +362,7 @@
         return p + pltpu.roll(p, KMAX // 2, 1)
 
     def substep(step, old, new, block):
-        ts = range(4 * block, 4 * block + 4)
+        ts = range(BLOCK * block, BLOCK * (block + 1))
         raw = [tt[t] if step == 0 else tt[t] + lap(old, t) for t in ts]
         z = product(jnp.concatenate(raw, axis=0), fwd)
         modes = []
@@ -367,7 +386,7 @@
             new[t] = g if step == 0 else old[t] + g
 
     for step, (old, new) in enumerate(((gb, ga), (ga, gb), (gb, ga))):
-        for block in range(WIN // 4):
+        for block in range(WIN // BLOCK):
             substep(step, old, new, block)
 
     for i in range(CHUNK):
@@ -379,7 +398,7 @@
         ret[:, p, :] = st[128 * p : 128 * (p + 1)].T
 
     def send_back(d):
-        return remote(ret.at[d], back.at[lon], b_s, b_r, at(d))
+        return remote(ret.at[d], back.at[lon], b_s, b_r.at[lon // PER], at(d))
 
     spread(send_back)
     back[lon] = ret[lon]
@@ -410,32 +429,41 @@
     def _(l):
         out[l, :, pl.ds(mid0, MW - 128)] = fm[l, 3 : 3 + SEG, pl.ds(own, MW - 128)]
 
-    total(b_r, back, SEGS - 1)
+    def store(l, first, lanes, half):
+        return pltpu.make_async_copy(
+            out.at[l, :, pl.ds(first, lanes)], out_hbm.at[:, l, pl.ds(first, lanes)], d_s.at[half, l]
+        )
+
+    stores = [store(l, rest0, ROWS - CW, 0) for l in range(LEV)]
+    for c in stores:
+        c.start()
     rl[:, CAP:CW] = jnp.zeros((LEV, CW - CAP, 128), F32)
-    lane128 = lax.broadcasted_iota(jnp.int32, (SEGS, 128), 1)
-    for i in range(CHUNK + 2):
-        p, off = divmod(SEG * i, 128)
-        r = back[:, p, :]
-        if off:
-            r = pltpu.roll(r, 128 - off, 1)
-        if off + SEG > 128:
-            r = jnp.where(lane128 < 128 - off, r, pltpu.roll(back[:, p + 1, :], 128 - off, 1))
-        for l in range(LEV):
+    lane128 = lax.broadcasted_iota(jnp.int32, (PER, 128), 1)
+    x = lane1 - lat * SHIFT
+    inside = jnp.logical_and(x >= 2 * lat, x < CAP + 2 + 2 * lat)
+    ends = []
+    for order, step in enumerate((0, 1, 3, 2)):
+        l = lax.rem(lon // PER + step, LEV)
+        total(b_r.at[l], back, PER - 1 if order == 0 else PER)
+        mine = back.at[pl.ds(pl.multiple_of(l * PER, PER), PER)]
+        for i in range(CHUNK + 2):
+            p, off = divmod(SEG * i, 128)
+            r = mine[:, p, :]
+            if off:
+                r = pltpu.roll(r, 128 - off, 1)
+            if off + SEG > 128:
+                r = jnp.where(lane128 < 128 - off, r, pltpu.roll(mine[:, p + 1, :], 128 - off, 1))
             if i < CHUNK:
-                rl[l, pl.ds(2 + i, PER, stride=CHUNK), :] = r[PER * l : PER * (l + 1)]
+                rl[order, pl.ds(2 + i, PER, stride=CHUNK), :] = r
             else:
-                rl[l, i - CHUNK : i - CHUNK + 1] = r[PER * l : PER * l + 1]
-                rl[l, CAP + 2 + i - CHUNK : CAP + 3 + i - CHUNK] = r[PER * (l + 1) - 1 : PER * (l + 1)]
-
-    stores = [pltpu.make_async_copy(out.at[l], out_hbm.at[:, l, :], d_s.at[l]) for l in range(LEV)]
-    for l in range(LEV):
-        add = jnp.concatenate([rl[l, 128 * b : 128 * (b + 1)].T[0:C8] for b in range(CW // 128)], axis=1)
+                rl[order, i - CHUNK : i - CHUNK + 1] = r[0:1]
+                rl[order, CAP + 2 + i - CHUNK : CAP + 3 + i - CHUNK] = r[PER - 1 : PER]
+        add = jnp.concatenate([rl[order, 128 * b : 128 * (b + 1)].T[0:C8] for b in range(CW // 128)], axis=1)
         add = pltpu.roll(add, lat * SHIFT, 1)[0:SEG]
-        x = lane1 - lat * SHIFT
-        inside = jnp.logical_and(x >= 2 * lat, x < CAP + 2 + 2 * lat)
         old = out[l, :, pl.ds(cap0, CW)]
         out[l, :, pl.ds(cap0, CW)] = jnp.where(inside, f[l, :, pl.ds(cap0, CW)] + add, old)
-        stores[l].start()
+        ends.append(store(l, cap0, CW, 1))
+        ends[-1].start()
 
     total(b_s, ret, SEGS - 1)
     for l in range(LEV):
@@ -445,37 +473,39 @@
         def _():
             c.wait_send()
 
-    for c in stores:
+    for c in stores + ends:
         c.wait()
 
 
 def body(f, u, v, cutoffs):
     cap_s, mid_s, rows_s = stretch_table()
-    vmem = pl.BlockSpec(memory_space=pltpu.VMEM)
-    smem = pl.BlockSpec(memory_space=pltpu.SMEM)
+    small = (cutoffs, rows_s, cap_s, mid_s) + tables()
     V = lambda *shape: pltpu.VMEM(shape, F32)
     dma = pltpu.SemaphoreType.DMA
     f, u, v = (jnp.transpose(a, (1, 0, 2)) for a in (f, u, v))
     done = pl.pallas_call(
         kernel,
         out_shape=jax.ShapeDtypeStruct(f.shape, F32),
-        in_specs=[pl.BlockSpec(memory_space=pl.ANY)] * 3 + [smem] * 2 + [vmem] * 5,
+        in_specs=[pl.BlockSpec(memory_space=pl.ANY)] * (3 + SMALL),
         out_specs=pl.BlockSpec(memory_space=pl.ANY),
         scratch_shapes=[
+            pltpu.SMEM(cutoffs.shape, jnp.int32), pltpu.SMEM(rows_s.shape, F32),
+            V(*cap_s.shape), V(*mid_s.shape),
+            pltpu.VMEM((256, 256), BF16), pltpu.VMEM((256, 256), BF16), V(4, C8, 128), dma((SMALL,)),
             V(LEV, SEG, ROWS), V(LEV, SEG, ROWS), V(LEV, SEG, ROWS), V(LEV, SEG, ROWS),
             V(LEV, 8, MW - 128), V(LEV, 8, MW - 128), V(LEV, 8, MW - 128), V(LEV, 8, MW - 128),
             V(LEV, 56, MW), V(LEV, 56, MW), V(LEV, 56, MW),
             V(136, CW), V(128, CW), V(CW, 128), V(CW, 128),
-            V(SEGS, WIN, 128), V(SEGS, WIN, 128), V(LEV, 8, 128), V(SEGS, 8, 128), V(3, 128, 128),
+            V(SEGS, WIN, 128), V(SEGS, WIN, 128), V(LEV, 2, 128), V(SEGS, 2, 128), V(3, 128, 128),
             V(WIN, C8, 128), V(WIN, C8, 128), V(WIN, C8, 128), V(WIN, C8, 128), V(WIN, C8, 128),
             V(128 * RET, 128), V(SEGS, RET, 128), V(SEGS, RET, 128), V(LEV, CW, 128),
-            dma((LEV,)), dma((3, LEV)), dma((3, LEV)), dma((2,)), dma((2,)), dma((3,)), dma((3,)),
-            dma, dma, dma((LEV,)), dma, dma, dma,
+            dma((2, LEV)), dma((3, LEV)), dma((3, LEV)), dma((2,)), dma((2,)), dma((3,)), dma((3,)),
+            dma, dma, dma((LEV,)), dma, dma, dma((LEV,)),
         ],
         compiler_params=pltpu.CompilerParams(
             collective_id=0, has_side_effects=True, vmem_limit_bytes=60 * 1024 * 1024
         ),
-    )(f, u, v, cutoffs, rows_s, cap_s, mid_s, *tables())
+    )(f, u, v, *small)
     return jnp.transpose(done, (1, 0, 2))
 
 

time: 58.1 us -> 56.2 us (0.967); the launches traced: 57.7 us -> 55.2 us
  Pallas kernels: 55.6 us -> 53.1 us
    pallas_call x1, Pallas kernels: 55.6 us -> 53.1 us  [body(): pl.pallas_call(kernel, out_shape=jax.ShapeDtypeStruct(f.shape, F32), in_s...]
where the time goes in v5:
time: 56.2 us; the launch traced here: 55.2 us
  Pallas kernels  53.1 us (94%)
  local copies, waits for them, and re-layouts  2.11 us (4%)
    pallas_call x1, Pallas kernels, body(): pl.pallas_call(kernel, out_shape=jax.ShapeDtypeStruct(f.shape, F32), in_s...  53.1 us
    unnamed x1, local copies, waits for them, and re-layouts  2.11 us

profile of v5, /device:TPU:8, one launch (start us, length us, event | category | flops | bytes accessed | tf_op | source)
XLA Modules:
  0.0 55.2 jit_solution(14701289559090270781)
XLA Ops:
  0.0 53.1 %shard_map.100 = f32[45,4,1152]{2,1,0:T(4,128)} custom-call(f32[45,4,1152]{2,1,0:T(4,128)} %bitcast.5, f32[45,4,1152]{2,1,0:T(4,128)} %bitcast.6, f32[45,4,1152]{2,1,0:T(4,128)} %bitcast.7, s32[2,384]{1,0:T(2,128)} %rest_0_.1, f32[2,388]{1,0:T(2,128)} %constant.12.clone.rest_1_, f32[2,1,512]{2,1,0:T(1,128)} %constant.13.clone.rest_2_, ...), custom_call_target="tpu_custom_call" | custom-call | tf_op jit(solution)/shard_map/pallas_call | solution.py:486
  53.1 2.1 %copy.12 = f32[4,45,1152]{2,0,1:T(4,128)} copy(f32[4,45,1152]{2,0,1:T(4,128)} %bitcast.4) | data formatting | bytes 1658880

commit v6 on v5

--- a/solution.py
+++ b/solution.py
@@ -230,9 +230,6 @@
 
         send(lax.rem(lon + SEGS // 2, SEGS)).start()
 
-    spread(send_line)
-    recv[lon] = msg[lon]
-
     def send_ext(l):
         d = l * PER + lat * (PER - 1)
         return d, remote(ext.at[l], ext_got.at[lon], x_s.at[l], x_r, at(d))
@@ -247,6 +244,9 @@
         @pl.when(d == lon)
         def _():
             ext_got[lon] = ext[l]
+
+    spread(send_line)
+    recv[lon] = msg[lon]
 
     for c in others:
         c.wait()

time: 56.2 us -> 55.4 us (0.986); the launches traced: 55.2 us -> 55.3 us
  no operation moved by 1% of the time
where the time goes in v6:
time: 55.4 us; the launch traced here: 55.3 us
  Pallas kernels  53.2 us (96%)
  local copies, waits for them, and re-layouts  2.11 us (4%)
    pallas_call x1, Pallas kernels, body(): pl.pallas_call(kernel, out_shape=jax.ShapeDtypeStruct(f.shape, F32), in_s...  53.2 us
    unnamed x1, local copies, waits for them, and re-layouts  2.11 us

profile of v6, /device:TPU:8, one launch (start us, length us, event | category | flops | bytes accessed | tf_op | source)
XLA Modules:
  0.0 55.3 jit_solution(78399595553824424)
XLA Ops:
  0.0 53.2 %shard_map.100 = f32[45,4,1152]{2,1,0:T(4,128)} custom-call(f32[45,4,1152]{2,1,0:T(4,128)} %bitcast.5, f32[45,4,1152]{2,1,0:T(4,128)} %bitcast.6, f32[45,4,1152]{2,1,0:T(4,128)} %bitcast.7, s32[2,384]{1,0:T(2,128)} %rest_0_.1, f32[2,388]{1,0:T(2,128)} %constant.12.clone.rest_1_, f32[2,1,512]{2,1,0:T(1,128)} %constant.13.clone.rest_2_, ...), custom_call_target="tpu_custom_call" | custom-call | tf_op jit(solution)/shard_map/pallas_call | solution.py:486
  53.2 2.1 %copy.12 = f32[4,45,1152]{2,0,1:T(4,128)} copy(f32[4,45,1152]{2,0,1:T(4,128)} %bitcast.4) | data formatting | bytes 1658880

commit v7 on v6

--- a/solution.py
+++ b/solution.py
@@ -281,61 +281,69 @@
     def total(sem, ref, n):
         pltpu.make_async_copy(ref.at[pl.ds(0, n)], ref.at[pl.ds(0, n)], sem).wait()
 
+    tt[:, SEG:C8] = jnp.zeros((WIN, C8 - SEG, 128), F32)
+    uu[:, SEG:C8] = jnp.zeros((WIN, C8 - SEG, 128), F32)
+    vv[:, SEG:C8] = jnp.zeros((WIN, C8 - SEG, 128), F32)
+    sp[2] = jnp.zeros((128, 128), F32)
+
+    @pl.when(jnp.logical_or(north_pole, south_pole))
+    def _():
+        total(x_r, ext_got, SEGS - 1)
+
+    @pl.when(north_pole)
+    def _():
+        sp[3] = ext_got[:, 0, :].T
+        sp[2] = ext_got[:, 1, :].T
+
+    @pl.when(south_pole)
+    def _():
+        sp[3] = ext_got[:, 1, :].T
+        sp[2] = ext_got[:, 0, :].T
+
     total(a_s, msg, SEGS - 1)
     for c in mids:
         c.start()
     total(a_r, recv, SEGS - 1)
-    tt[:, SEG:C8] = jnp.zeros((WIN, C8 - SEG, 128), F32)
-    uu[:, SEG:C8] = jnp.zeros((WIN, C8 - SEG, 128), F32)
-    vv[:, SEG:C8] = jnp.zeros((WIN, C8 - SEG, 128), F32)
     for t in range(WIN):
         w = recv[:, t, :].T
         tt[t, 0:SEG] = w[0:SEG]
-        uu[t, 0:SEG] = w[SEG : 2 * SEG]
-        vv[t, 0 : SEG - TAIL] = w[2 * SEG : 128]
+        uu[t, 0:SEG] = (-0.05 * rows_s[lat, CHUNK * jj + t]) * w[SEG : 2 * SEG]
+        vv[t, 0 : SEG - TAIL] = -0.05 * w[2 * SEG : 128]
         if t == 0:
             sp[0] = w
         if t == WIN - 1:
             sp[1] = w
 
-    @pl.when(jnp.logical_or(north_pole, south_pole))
-    def _():
-        total(x_r, ext_got, SEGS - 1)
-
-    sp[2] = jnp.zeros((128, 128), F32)
-
     @pl.when(north_pole)
     def _():
-        sp[0] = ext_got[:, 0, :].T
-        sp[2] = ext_got[:, 1, :].T
+        sp[0] = sp[3]
 
     @pl.when(south_pole)
     def _():
-        sp[1] = ext_got[:, 1, :].T
-        sp[2] = ext_got[:, 0, :].T
+        sp[1] = sp[3]
 
     for i in range(8):
         t0 = i + 1 if i < 7 else 15
         t15 = i + 8 if i < 7 else 0
         lo, hi = SEG + TAIL * i, SEG + TAIL * (i + 1)
-        vv[t0, SEG - TAIL : SEG] = sp[0, lo:hi]
-        vv[t15, SEG - TAIL : SEG] = sp[1, lo:hi]
+        vv[t0, SEG - TAIL : SEG] = -0.05 * sp[0, lo:hi]
+        vv[t15, SEG - TAIL : SEG] = -0.05 * sp[1, lo:hi]
 
     e_in = pltpu.roll(sp[0, COLS - 5 : COLS + 19], 127, 1)
     w_in = pltpu.roll(sp[1, COLS - 5 : COLS + 19], 1, 1)
     for t in range(WIN):
         sw = rows_s[lat, CHUNK * jj + t]
         if t in (0, WIN - 1):
-            u0 = sp[t // (WIN - 1), COLS + WIN : COLS + WIN + 1]
-            u44 = sp[t // (WIN - 1), COLS + WIN + 1 : COLS + WIN + 2]
+            u0 = (-0.05 * sw) * sp[t // (WIN - 1), COLS + WIN : COLS + WIN + 1]
+            u44 = (-0.05 * sw) * sp[t // (WIN - 1), COLS + WIN + 1 : COLS + WIN + 2]
         else:
             u0, u44 = uu[t, 0:1], uu[t, SEG - 1 : SEG]
         r = 5 + 15 - t
-        tt[t, SEG - 1 : SEG] += (0.02 * sw - 0.05 * sw * u44) * e_in[r : r + 1]
-        tt[t, 0:1] += (0.02 * sw + 0.05 * sw * u0) * w_in[r : r + 1]
-    opp = 0.05 * pltpu.roll(sp[2, 0:C8], SEGS // 2, 1)[:SEG]
-    tt[0, 0:SEG] -= jnp.where(north_pole, vv[0, 0:SEG] * opp, 0.0)
-    tt[WIN - 1, 0:SEG] += jnp.where(south_pole, vv[WIN - 1, 0:SEG] * opp, 0.0)
+        tt[t, SEG - 1 : SEG] += (0.02 * sw + u44) * e_in[r : r + 1]
+        tt[t, 0:1] += (0.02 * sw - u0) * w_in[r : r + 1]
+    opp = pltpu.roll(sp[2, 0:C8], SEGS // 2, 1)[:SEG]
+    tt[0, 0:SEG] += jnp.where(north_pole, vv[0, 0:SEG] * opp, 0.0)
+    tt[WIN - 1, 0:SEG] -= jnp.where(south_pole, vv[WIN - 1, 0:SEG] * opp, 0.0)
 
     col = lax.broadcasted_iota(jnp.int32, (C8, 128), 0)
     m_lane = lax.rem(lax.broadcasted_iota(jnp.int32, (1, KMAX), 1), KMAX // 2)
@@ -355,7 +363,7 @@
             n = jnp.where(north_pole, pltpu.roll(g, SEGS // 2, 1), n)
         if t == WIN - 1:
             s = jnp.where(south_pole, pltpu.roll(g, SEGS // 2, 1), s)
-        return tend(g, e, w, n, s, uu[t], vv[t], rows_s[lat, CHUNK * jj + t])
+        return uu[t] * (e - w) + vv[t] * (n - s) + (0.02 * rows_s[lat, CHUNK * jj + t]) * (e - 2.0 * g + w)
 
     def fold(z, table):
         p = jnp.sum(z * table, axis=0, keepdims=True)
@@ -496,7 +504,7 @@
             V(LEV, 8, MW - 128), V(LEV, 8, MW - 128), V(LEV, 8, MW - 128), V(LEV, 8, MW - 128),
             V(LEV, 56, MW), V(LEV, 56, MW), V(LEV, 56, MW),
             V(136, CW), V(128, CW), V(CW, 128), V(CW, 128),
-            V(SEGS, WIN, 128), V(SEGS, WIN, 128), V(LEV, 2, 128), V(SEGS, 2, 128), V(3, 128, 128),
+            V(SEGS, WIN, 128), V(SEGS, WIN, 128), V(LEV, 2, 128), V(SEGS, 2, 128), V(4, 128, 128),
             V(WIN, C8, 128), V(WIN, C8, 128), V(WIN, C8, 128), V(WIN, C8, 128), V(WIN, C8, 128),
             V(128 * RET, 128), V(SEGS, RET, 128), V(SEGS, RET, 128), V(LEV, CW, 128),
             dma((2, LEV)), dma((3, LEV)), dma((3, LEV)), dma((2,)), dma((2,)), dma((3,)), dma((3,)),

time: 55.4 us -> 55.4 us (level)
  no operation moved by 1% of the time
where the time goes in v7:
time: 55.4 us; the launch traced here: 55.3 us
  Pallas kernels  53.2 us (96%)
  local copies, waits for them, and re-layouts  2.11 us (4%)
    pallas_call x1, Pallas kernels, body(): pl.pallas_call(kernel, out_shape=jax.ShapeDtypeStruct(f.shape, F32), in_s...  53.2 us
    unnamed x1, local copies, waits for them, and re-layouts  2.11 us

profile of v7, /device:TPU:8, one launch (start us, length us, event | category | flops | bytes accessed | tf_op | source)
XLA Modules:
  0.0 55.3 jit_solution(16474642256979407320)
XLA Ops:
  0.0 53.2 %shard_map.100 = f32[45,4,1152]{2,1,0:T(4,128)} custom-call(f32[45,4,1152]{2,1,0:T(4,128)} %bitcast.5, f32[45,4,1152]{2,1,0:T(4,128)} %bitcast.6, f32[45,4,1152]{2,1,0:T(4,128)} %bitcast.7, s32[2,384]{1,0:T(2,128)} %rest_0_.1, f32[2,388]{1,0:T(2,128)} %constant.12.clone.rest_1_, f32[2,1,512]{2,1,0:T(1,128)} %constant.13.clone.rest_2_, ...), custom_call_target="tpu_custom_call" | custom-call | tf_op jit(solution)/shard_map/pallas_call | solution.py:494
  53.2 2.1 %copy.12 = f32[4,45,1152]{2,0,1:T(4,128)} copy(f32[4,45,1152]{2,0,1:T(4,128)} %bitcast.4) | data formatting | bytes 1658880

commit v8 on v6

--- a/solution.py
+++ b/solution.py
@@ -128,13 +128,14 @@
     def greet(k):
         pl.semaphore_signal(barrier, inc=1, device_id=at(lax.rem(lon + k, SEGS)), device_id_type=MESH)
 
-    @pl.loop(0, (SEGS - 1) // 8)
+    greet(SEGS // 2)
+
+    @pl.loop(0, (SEGS // 2 - 1) // 7)
     def _(k):
-        for i in range(8):
-            greet(8 * k + i + 1)
-
-    for k in range((SEGS - 1) // 8 * 8 + 1, SEGS):
-        greet(k)
+        for i in range(1, 8):
+            greet(SEGS // 2 - 7 * k - i)
+            greet(SEGS // 2 + 7 * k + i)
+
     pl.semaphore_signal(barrier, inc=1, device_id=partner, device_id_type=MESH)
 
     held = (cuts, rows_s, cap_s, mid_s, fwd, inv, twiddle)

time: 55.4 us -> 55.6 us (level); the launches traced: 55.3 us -> 54.8 us
  no operation moved by 1% of the time
where the time goes in v8:
time: 55.6 us; the launch traced here: 54.8 us
  Pallas kernels  52.7 us (95%)
  local copies, waits for them, and re-layouts  2.11 us (4%)
    pallas_call x1, Pallas kernels, body(): pl.pallas_call(kernel, out_shape=jax.ShapeDtypeStruct(f.shape, F32), in_s...  52.7 us
    unnamed x1, local copies, waits for them, and re-layouts  2.11 us

profile of v8, /device:TPU:8, one launch (start us, length us, event | category | flops | bytes accessed | tf_op | source)
XLA Modules:
  0.0 54.8 jit_solution(11770589186414216159)
XLA Ops:
  0.0 52.7 %shard_map.100 = f32[45,4,1152]{2,1,0:T(4,128)} custom-call(f32[45,4,1152]{2,1,0:T(4,128)} %bitcast.5, f32[45,4,1152]{2,1,0:T(4,128)} %bitcast.6, f32[45,4,1152]{2,1,0:T(4,128)} %bitcast.7, s32[2,384]{1,0:T(2,128)} %rest_0_.1, f32[2,388]{1,0:T(2,128)} %constant.12.clone.rest_1_, f32[2,1,512]{2,1,0:T(1,128)} %constant.13.clone.rest_2_, ...), custom_call_target="tpu_custom_call" | custom-call | tf_op jit(solution)/shard_map/pallas_call | solution.py:487
  52.7 2.1 %copy.12 = f32[4,45,1152]{2,0,1:T(4,128)} copy(f32[4,45,1152]{2,0,1:T(4,128)} %bitcast.4) | data formatting | bytes 1658880
